TPU v7x, 1024 devices: a whole 4x4x32 slice. The times are simulated.
1024 devices in a mesh: space: 256 (over x, z, core), band: 4 (over y).
Axes of the slice: x: 4, y: 4, z: 32, core: 2. Of those that a mesh axis runs over, the one named last changes fastest.
Arguments:
- wave_in: bfloat16 [4096, 16, 16, 512], P('space', None, None, 'band'), parts along dimension 3, may hold values from -6 to 6
- mass_scale: float32 [4096, 256], P('space'), may hold values from 0.5 to 1
- potential: float32 [4096, 256], P('space'), may hold values from -2 to 1
- elem_scale: float32 [512, 2, 2], P('space'), may hold values from 0.5 to 1.5
- stiffness: bfloat16 [729, 729], replicated, as said below
- proj_lower: bfloat16 [256, 729, 32], P('space'), may hold values from -0.21875 to 0.21875
- proj_upper: bfloat16 [256, 729, 32], P('space'), may hold values from -0.21875 to 0.21875
- kb_coef: float32 [256, 32], P('space'), may hold values from -3 to 3
- atom_column: int32 [256], P('space'), may hold values from 0 to 3
- chan_count: int32 [256], P('space'), may hold values from 8 to 32
- upper_column: int32 [256], P('space'), may hold values from 0 to 3
Outputs:
- filtered: bfloat16 [4096, 16, 16, 512], P('space', None, None, 'band'), parts along dimension 3
- coefficients: float32 [256, 32, 512], P('space', None, 'band'), parts along dimension 2
There are 4 independent parts, one for each index of `band`. A program takes and returns all parts, laid end to end along the dimension named above; an argument that names none is the same for every part. Nothing has to cross between parts.
Inputs may be any that keep to these rules, and one draw needn't show every extreme that they name: stiffness is symmetric.
All inputs are finite; a program needn't handle non-finite values.
Results may differ from a plain program's by a relative error of at most 0.006.
Values may be sent and summed in bfloat16 or wider, within the bound.
A program may use at most 32 MiB of HBM per device.

v0:
```python
import jax
import jax.numpy as jnp
from jax import lax
from jax.sharding import PartitionSpec as P

spectrum_center = 1.0
spectrum_half = 6.0
highest = lax.Precision.HIGHEST


def shifted(value, axis, steps):
    count = lax.axis_size(axis)
    pairs = [(source, (source + steps) % count) for source in range(count)]
    return lax.ppermute(value, axis, pairs)


def wrap_sides(planes):
    planes = jnp.concatenate([planes, planes[:, :1]], axis=1)
    return jnp.concatenate([planes, planes[:, :, :1]], axis=2)


def layer_blocks(layer_nodes, degree):
    points = degree + 1
    gathered = []
    for across in range(2):
        for column in range(2):
            portion = layer_nodes[
                :,
                across * degree : across * degree + points,
                column * degree : column * degree + points,
            ]
            gathered.append(portion.reshape(points * points * points, layer_nodes.shape[-1]))
    return jnp.stack(gathered)


def cut_piece(values, start, stop, axis):
    return lax.slice_in_dim(values, start, stop, axis=axis)


def join_pair(lower, upper, axis, wrapped, degree):
    first = cut_piece(lower, 0, 1, axis)
    if wrapped:
        first = first + cut_piece(upper, degree, degree + 1, axis)
    middle = cut_piece(lower, degree, degree + 1, axis) + cut_piece(upper, 0, 1, axis)
    pieces = [first, cut_piece(lower, 1, degree, axis), middle, cut_piece(upper, 1, degree, axis)]
    if not wrapped:
        pieces.append(cut_piece(upper, degree, degree + 1, axis))
    return jnp.concatenate(pieces, axis=axis)


def assemble_blocks(results, degree):
    points = degree + 1
    band_count = results.shape[-1]
    grouped = results.reshape(2, 2, 2, points, points, points, band_count)
    joined_columns = join_pair(grouped[:, :, 0], grouped[:, :, 1], 4, True, degree)
    joined_across = join_pair(joined_columns[:, 0], joined_columns[:, 1], 2, True, degree)
    return join_pair(joined_across[0], joined_across[1], 0, False, degree)


def split_layers(nodal_field, degree):
    upper_rim = shifted(nodal_field[:1], "space", -1)
    bottom_blocks = layer_blocks(wrap_sides(nodal_field[: degree + 1]), degree)
    top_blocks = layer_blocks(
        wrap_sides(jnp.concatenate([nodal_field[degree:], upper_rim], axis=0)), degree
    )
    return (bottom_blocks, top_blocks)


def column_onehot(columns):
    return (columns[:, None] == jnp.arange(4, dtype=jnp.int32)[None, :]).astype(jnp.float32)


def projections(projector, blocks, columns):
    every_column = jnp.einsum(
        "anc,knb->akcb", projector, blocks, preferred_element_type=jnp.float32
    )
    return jnp.einsum("ak,akcb->acb", column_onehot(columns), every_column, precision=highest)


def scatter_columns(projector, coef_block, columns):
    placed = (
        column_onehot(columns).astype(jnp.bfloat16)[:, :, None, None] * coef_block[:, None, :, :]
    )
    return jnp.einsum("anc,akcb->knb", projector, placed, preferred_element_type=jnp.float32)


def gather_partials(bottom_blocks, top_blocks, proj_lower, proj_upper, atom_column, upper_column):
    held_part = projections(proj_upper, bottom_blocks, upper_column)
    incoming = shifted(held_part, "space", -1)
    own_part = projections(proj_lower, top_blocks, atom_column)
    return (held_part, own_part, incoming)


def per_device(
    wave_in,
    mass_scale,
    potential,
    elem_scale,
    stiffness,
    proj_lower,
    proj_upper,
    kb_coef,
    atom_column,
    chan_count,
    upper_column,
):
    extent = wave_in.shape[0]
    degree = extent // 2
    channels = kb_coef.shape[-1]
    mass_nodes = mass_scale.reshape(extent, extent, extent, 1)
    local_potential = potential.reshape(extent, extent, extent, 1)
    scales = elem_scale.reshape(8)
    live_channels = (jnp.arange(channels, dtype=jnp.int32)[None, :] < chan_count[:, None]).astype(
        jnp.float32
    )
    weights = kb_coef * live_channels

    def operator(nodal_field):
        bottom_blocks, top_blocks = split_layers(nodal_field, degree)
        held_part, own_part, incoming = gather_partials(
            bottom_blocks, top_blocks, proj_lower, proj_upper, atom_column, upper_column
        )
        own_coef = ((own_part + incoming) * weights[:, :, None]).astype(jnp.bfloat16)
        below_coef = shifted(own_coef, "space", 1)
        local_bottom = (
            jnp.einsum("ij,ejb->eib", stiffness, bottom_blocks, preferred_element_type=jnp.float32)
            * scales[:4, None, None]
        )
        local_top = (
            jnp.einsum("ij,ejb->eib", stiffness, top_blocks, preferred_element_type=jnp.float32)
            * scales[4:, None, None]
        )
        results = jnp.concatenate(
            [
                local_bottom + scatter_columns(proj_upper, below_coef, upper_column),
                local_top + scatter_columns(proj_lower, own_coef, atom_column),
            ]
        )
        summed = assemble_blocks(results, degree)
        received = shifted(summed[-1], "space", 1)
        assembled = jnp.concatenate([summed[:1] + received[None], summed[1:-1]], axis=0)
        return mass_nodes * (assembled + local_potential * nodal_field.astype(jnp.float32))

    initial = wave_in.astype(jnp.float32)
    scaled_start = (mass_nodes * initial).astype(jnp.bfloat16)
    image_one = operator(scaled_start)
    step_one = ((image_one - spectrum_center * initial) / spectrum_half).astype(jnp.bfloat16)
    scaled_step = (mass_nodes * step_one.astype(jnp.float32)).astype(jnp.bfloat16)
    image_two = operator(scaled_step)
    filtered = (
        2.0 * (image_two - spectrum_center * step_one.astype(jnp.float32)) / spectrum_half - initial
    ).astype(jnp.bfloat16)
    bottom_blocks, top_blocks = split_layers(filtered, degree)
    held_part, own_part, incoming = gather_partials(
        bottom_blocks, top_blocks, proj_lower, proj_upper, atom_column, upper_column
    )
    coefficients = own_part + incoming
    return (filtered, coefficients)


def solution(mesh):
    in_specs = (
        P("space", None, None, "band"),
        P("space", None),
        P("space", None),
        P("space", None, None),
        P(),
        P("space", None, None),
        P("space", None, None),
        P("space", None),
        P("space"),
        P("space"),
        P("space"),
    )
    out_specs = (P("space", None, None, "band"), P("space", None, "band"))
    return jax.shard_map(
        per_device, mesh=mesh, in_specs=in_specs, out_specs=out_specs, check_vma=False
    )
```

profile of v0, /device:TPU:1, one launch (start us, length us, event | category | flops | bytes accessed | tf_op | source)
XLA Modules:
  0.0 148.6 jit_solution(3305100937003875141)
XLA Ops:
  1.6 1.8 %fusion.2 = bf16[16,16,16,128]{3,2,1,0:T(8,128)(2,1)S(1)} fusion(bf16[16,16,16,128]{3,2,1,0:T(8,128)(2,1)} %param.11, f32[16,16,16]{2,1,0:T(8,128)S(1)} %mul.169), kind=kLoop, calls=%fused_computation.15 | loop fusion | flops 1572864 | bytes 2113536 | tf_op jit(solution)/shard_map/convert_element_type | solution.py:145
  3.9 16.1 %collective-permute-start = (bf16[1,16,16,128]{3,2,1,0:T(8,128)(2,1)}, bf16[1,16,16,128]{3,2,1,0:T(8,128)(2,1)S(1)}, u32[]{:S(2)}, u32[]{:S(2)}) collective-permute-start(bf16[1,16,16,128]{3,2,1,0:T(8,128)(2,1)} %slice.424), channel_id=1, source_target_pairs={{0,1020},{4,0},{8,4},{12,8},{16,12},{20,16},{24,20},{28,24},{32,28... | collective-permute-start | bytes 196616 | tf_op jit(solution)/shard_map/ppermute | solution.py:14
  21.5 1.9 %fusion.38 = (bf16[9,9,9,128]{3,2,1,0:T(8,128)(2,1)}, bf16[9,9,9,128]{3,2,1,0:T(8,128)(2,1)}, bf16[9,9,9,128]{3,2,1,0:T(8,128)(2,1)S(1)}) fusion(bf16[9,1,16,128]{3,2,1,0:T(8,128)(2,1)} %slice.422, bf16[9,16,16,128]{3,2,1,0:T(8,128)(2,1)S(1)} %slice.421), kind=kLoop, calls=%fused_computation.104 | loop fusion | flops 1866240 | bytes 1186560 | tf_op jit(solution)/shard_map/concatenate | solution.py:19
  26.7 7.7 %collective-permute-start.1 = (f32[1,32,128]{2,1,0:T(8,128)S(1)}, f32[1,32,128]{2,1,0:T(8,128)S(1)}, u32[]{:S(2)}, u32[]{:S(2)}) collective-permute-start(f32[1,32,128]{2,1,0:T(8,128)S(1)} %bitcast.216), channel_id=1, source_target_pairs={{0,1020},{4,0},{8,4},{12,8},{16,12},{20,16},{24,20},{28,24},{32,28... | collective-permute-start | bytes 49160 | tf_op jit(solution)/shard_map/ppermute | solution.py:14
  36.6 3.0 %fusion.14 = f32[4,128,729]{1,2,0:T(8,128)} fusion(bf16[4,729,128]{2,1,0:T(8,128)(2,1)} %copy-done.12, bf16[729,729]{1,0:T(8,128)(2,1)S(1)} %copy-done), kind=kOutput, calls=%fused_computation.35 | convolution fusion | flops 544195584 | bytes 3302370 | tf_op jit(solution)/shard_map/ij,ejb->eib/dot_general | solution.py:126
  41.8 2.1 %collective-permute-start.2 = (bf16[1,32,128]{2,1,0:T(8,128)(2,1)S(1)}, bf16[1,32,128]{2,1,0:T(8,128)(2,1)S(1)}, u32[]{:S(2)}, u32[]{:S(2)}) collective-permute-start(bf16[1,32,128]{2,1,0:T(8,128)(2,1)S(1)} %multiply_convert_fusion.1), channel_id=1, source_target_pairs={{0,4},{4,8},{8,12},{12,16},{16,20},{20,24},{24,28},{28,32},{32,36}... | collective-permute-start | bytes 24584 | tf_op jit(solution)/shard_map/ppermute | solution.py:14
  45.7 1.7 %copy.17 = f32[8,729,128]{2,0,1:T(8,128)S(1)} copy(f32[8,729,128]{2,1,0:T(8,128)S(1)} %pad_maximum_fusion) | data formatting | bytes 5971968 | tf_op jit(solution)/shard_map/concatenate | solution.py:133
  47.4 2.3 %fusion.94 = (f32[2,2,1,9,9,9,128]{6,2,1,0,5,4,3:T(1,128)S(1)}, f32[2,2,1,9,9,9,128]{6,2,1,0,5,4,3:T(1,128)S(1)}) fusion(f32[2,2,2,9,9,9,128]{6,2,1,0,5,4,3:T(2,128)S(1)} %bitcast.193), kind=kLoop, calls=%fused_computation.206 | loop fusion | bytes 5971968 | tf_op jit(solution)/shard_map/slice | solution.py:55
  52.3 3.0 %fusion.95 = (f32[2,1,9,9,16,128]{5,1,0,4,3,2:T(1,128)S(1)}, f32[2,1,9,9,16,128]{5,1,0,4,3,2:T(1,128)S(1)}) fusion(f32[2,2,9,9,16,128]{5,1,0,4,3,2:T(2,128)S(1)} %pad_maximum_fusion.2), kind=kLoop, calls=%fused_computation.207 | loop fusion | bytes 5308416 | tf_op jit(solution)/shard_map/slice | solution.py:56
  58.6 4.0 %collective-permute-start.3 = (f32[16,16,128]{2,1,0:T(8,128)S(1)}, f32[16,16,128]{2,1,0:T(8,128)S(1)}, u32[]{:S(2)}, u32[]{:S(2)}) collective-permute-start(f32[16,16,128]{2,1,0:T(8,128)S(1)} %bitcast.210), channel_id=1, source_target_pairs={{0,4},{4,8},{8,12},{12,16},{16,20},{20,24},{24,28},{28,32},{32,36}... | collective-permute-start | bytes 393224 | tf_op jit(solution)/shard_map/ppermute | solution.py:14
  63.4 3.9 %collective-permute-done.3 = f32[16,16,128]{2,1,0:T(8,128)S(1)} collective-permute-done((f32[16,16,128]{2,1,0:T(8,128)S(1)}, f32[16,16,128]{2,1,0:T(8,128)S(1)}, u32[]{:S(2)}, u32[]{:S(2)}) %collective-permute-start.3) | collective-permute-done | bytes 131104 | tf_op jit(solution)/shard_map/ppermute | solution.py:14
  71.7 1.7 %stack_reshape.80 = bf16[1,729,128]{2,1,0:T(8,128)(2,1)} reshape(bf16[9,9,9,128]{3,2,1,0:T(8,128)(2,1)} %slice.444) | data formatting | bytes 373248 | tf_op jit(solution)/shard_map/stack;reshape | solution.py:33
  73.5 2.4 %fusion.36 = (bf16[9,9,9,128]{3,2,1,0:T(8,128)(2,1)}, bf16[9,9,9,128]{3,2,1,0:T(8,128)(2,1)}, bf16[9,9,9,128]{3,2,1,0:T(8,128)(2,1)}) fusion(bf16[9,1,16,128]{3,2,1,0:T(8,128)(2,1)} %slice.446, bf16[9,16,16,128]{3,2,1,0:T(8,128)(2,1)} %slice.445), kind=kLoop, calls=%fused_computation.91 | loop fusion | flops 1866240 | bytes 1186560 | tf_op jit(solution)/shard_map/concatenate | solution.py:19
  75.8 1.7 %stack_reshape.83 = bf16[1,729,128]{2,1,0:T(8,128)(2,1)} reshape(bf16[9,9,9,128]{3,2,1,0:T(8,128)(2,1)} %get-tuple-element.30) | data formatting | bytes 373248 | tf_op jit(solution)/shard_map/stack;reshape | solution.py:33
  77.6 1.7 %stack_reshape.81 = bf16[1,729,128]{2,1,0:T(8,128)(2,1)} reshape(bf16[9,9,9,128]{3,2,1,0:T(8,128)(2,1)} %get-tuple-element.31) | data formatting | bytes 373248 | tf_op jit(solution)/shard_map/stack;reshape | solution.py:33
  79.3 1.7 %stack_reshape.82 = bf16[1,729,128]{2,1,0:T(8,128)(2,1)} reshape(bf16[9,9,9,128]{3,2,1,0:T(8,128)(2,1)} %get-tuple-element.32) | data formatting | bytes 373248 | tf_op jit(solution)/shard_map/stack;reshape | solution.py:33
  85.1 1.9 %fusion.10 = f32[4,128,729]{1,2,0:T(8,128)} fusion(bf16[4,729,128]{2,1,0:T(8,128)(2,1)S(1)} %constant_dynamic-update-slice_fusion.8, bf16[729,729]{1,0:T(8,128)(2,1)S(1)} %copy-done), kind=kOutput, calls=%fused_computation.31 | convolution fusion | flops 544195584 | bytes 3302370 | tf_op jit(solution)/shard_map/ij,ejb->eib/dot_general | solution.py:126
  87.0 8.8 %collective-permute-start.4 = (bf16[1,16,16,128]{3,2,1,0:T(8,128)(2,1)S(1)}, bf16[1,16,16,128]{3,2,1,0:T(8,128)(2,1)S(1)}, u32[]{:S(2)}, u32[]{:S(2)}) collective-permute-start(bf16[1,16,16,128]{3,2,1,0:T(8,128)(2,1)S(1)} %copy-done.17), channel_id=1, source_target_pairs={{0,1020},{4,0},{8,4},{12,8},{16,12},{20,16},{24,20},{28,24},{32,28... | collective-permute-start | bytes 196616 | tf_op jit(solution)/shard_map/ppermute | solution.py:14
  96.1 1.9 %collective-permute-start.5 = (f32[1,32,128]{2,1,0:T(8,128)S(1)}, f32[1,32,128]{2,1,0:T(8,128)}, u32[]{:S(2)}, u32[]{:S(2)}) collective-permute-start(f32[1,32,128]{2,1,0:T(8,128)S(1)} %bitcast.217), channel_id=1, source_target_pairs={{0,1020},{4,0},{8,4},{12,8},{16,12},{20,16},{24,20},{28,24},{32,28... | collective-permute-start | bytes 49160 | tf_op jit(solution)/shard_map/ppermute | solution.py:14
  99.1 1.7 %stack_reshape.87 = bf16[1,729,128]{2,1,0:T(8,128)(2,1)} reshape(bf16[9,9,9,128]{3,2,1,0:T(8,128)(2,1)} %get-tuple-element.33) | data formatting | bytes 373248 | tf_op jit(solution)/shard_map/stack;reshape | solution.py:33
  100.9 1.8 %stack_reshape.86 = bf16[1,729,128]{2,1,0:T(8,128)(2,1)} reshape(bf16[9,9,9,128]{3,2,1,0:T(8,128)(2,1)} %get-tuple-element.34) | data formatting | bytes 373248 | tf_op jit(solution)/shard_map/stack;reshape | solution.py:33
  102.6 1.7 %stack_reshape.85 = bf16[1,729,128]{2,1,0:T(8,128)(2,1)} reshape(bf16[9,9,9,128]{3,2,1,0:T(8,128)(2,1)} %get-tuple-element.35) | data formatting | bytes 373248 | tf_op jit(solution)/shard_map/stack;reshape | solution.py:33
  104.4 1.7 %stack_reshape.84 = bf16[1,729,128]{2,1,0:T(8,128)(2,1)} reshape(bf16[9,9,9,128]{3,2,1,0:T(8,128)(2,1)} %get-tuple-element.43) | data formatting | bytes 373248 | tf_op jit(solution)/shard_map/stack;reshape | solution.py:33
  113.0 3.6 %collective-permute-start.6 = (bf16[1,32,128]{2,1,0:T(8,128)(2,1)S(1)}, bf16[1,32,128]{2,1,0:T(8,128)(2,1)S(1)}, u32[]{:S(2)}, u32[]{:S(2)}) collective-permute-start(bf16[1,32,128]{2,1,0:T(8,128)(2,1)S(1)} %multiply_convert_fusion), channel_id=1, source_target_pairs={{0,4},{4,8},{8,12},{12,16},{16,20},{20,24},{24,28},{28,32},{32,36}... | collective-permute-start | bytes 24584 | tf_op jit(solution)/shard_map/ppermute | solution.py:14
  118.0 1.7 %copy.25 = f32[8,729,128]{2,0,1:T(8,128)S(1)} copy(f32[8,729,128]{2,1,0:T(8,128)S(1)} %pad_maximum_fusion.1) | data formatting | bytes 5971968 | tf_op jit(solution)/shard_map/concatenate | solution.py:133
  119.8 2.3 %fusion.93 = (f32[2,2,1,9,9,9,128]{6,2,1,0,5,4,3:T(1,128)S(1)}, f32[2,2,1,9,9,9,128]{6,2,1,0,5,4,3:T(1,128)S(1)}) fusion(f32[2,2,2,9,9,9,128]{6,2,1,0,5,4,3:T(2,128)S(1)} %bitcast.194), kind=kLoop, calls=%fused_computation.205 | loop fusion | bytes 5971968 | tf_op jit(solution)/shard_map/slice | solution.py:55
  124.7 4.2 %collective-permute-start.7 = (f32[16,16,128]{2,1,0:T(8,128)S(1)}, f32[16,16,128]{2,1,0:T(8,128)S(1)}, u32[]{:S(2)}, u32[]{:S(2)}) collective-permute-start(f32[16,16,128]{2,1,0:T(8,128)S(1)} %get-tuple-element.18), channel_id=1, source_target_pairs={{0,4},{4,8},{8,12},{12,16},{16,20},{20,24},{24,28},{28,32},{32,36}... | collective-permute-start | bytes 393224 | tf_op jit(solution)/shard_map/ppermute | solution.py:14
  129.0 2.3 %collective-permute-done.7 = f32[16,16,128]{2,1,0:T(8,128)S(1)} collective-permute-done((f32[16,16,128]{2,1,0:T(8,128)S(1)}, f32[16,16,128]{2,1,0:T(8,128)S(1)}, u32[]{:S(2)}, u32[]{:S(2)}) %collective-permute-start.7) | collective-permute-done | bytes 131104 | tf_op jit(solution)/shard_map/ppermute | solution.py:14
  131.3 1.5 %fusion.5 = bf16[16,16,16,128]{3,2,1,0:T(8,128)(2,1)S(1)} fusion(bf16[16,16,16,128]{3,2,1,0:T(8,128)(2,1)S(1)} %copy-done.2, f32[7,16,16,128]{3,2,1,0:T(8,128)S(1)} %maximum_bitcast_fusion, f32[1,16,16,128]{3,2,1,0:T(8,128)S(1)} %get-tuple-element.19, f32[7,16,16,128]{3,2,1,0:T(8,128)S(1)} %slice_bitcast_fusion.2, f32[1,16,16,128]{3,2,1,0:T(8,128)S(1)} %fusion.41, ...), kind=kLoop, calls=%fused_computation.18 | loop fusion | flops 14155776 | bytes 6324224 | tf_op jit(solution)/shard_map/convert_element_type | solution.py:152
  133.1 8.8 %collective-permute-start.8 = (bf16[1,16,16,128]{3,2,1,0:T(8,128)(2,1)S(1)}, bf16[1,16,16,128]{3,2,1,0:T(8,128)(2,1)S(1)}, u32[]{:S(2)}, u32[]{:S(2)}) collective-permute-start(bf16[1,16,16,128]{3,2,1,0:T(8,128)(2,1)S(1)} %slice.469), channel_id=1, source_target_pairs={{0,1020},{4,0},{8,4},{12,8},{16,12},{20,16},{24,20},{28,24},{32,28... | collective-permute-start | bytes 196616 | tf_op jit(solution)/shard_map/ppermute | solution.py:14
  142.9 1.9 %collective-permute-start.9 = (f32[1,32,128]{2,1,0:T(8,128)S(1)}, f32[1,32,128]{2,1,0:T(8,128)S(1)}, u32[]{:S(2)}, u32[]{:S(2)}) collective-permute-start(f32[1,32,128]{2,1,0:T(8,128)S(1)} %bitcast.218), channel_id=1, source_target_pairs={{0,1020},{4,0},{8,4},{12,8},{16,12},{20,16},{24,20},{28,24},{32,28... | collective-permute-start | bytes 49160 | tf_op jit(solution)/shard_map/ppermute | solution.py:14
  146.1 1.8 %collective-permute-done.9 = f32[1,32,128]{2,1,0:T(8,128)S(1)} collective-permute-done((f32[1,32,128]{2,1,0:T(8,128)S(1)}, f32[1,32,128]{2,1,0:T(8,128)S(1)}, u32[]{:S(2)}, u32[]{:S(2)}) %collective-permute-start.9) | collective-permute-done | bytes 16416 | tf_op jit(solution)/shard_map/ppermute | solution.py:14
  (182 shorter events, 40.4 us)
Async XLA Ops:
  0.6 36.0 %copy-start = (bf16[729,729]{1,0:T(8,128)(2,1)S(1)}, bf16[729,729]{1,0:T(8,128)(2,1)}, u32[]{:S(2)}) copy-start(bf16[729,729]{1,0:T(8,128)(2,1)} %param.15) | copy-start | bytes 3188650
  3.9 35.8 %collective-permute-start = (bf16[1,16,16,128]{3,2,1,0:T(8,128)(2,1)}, bf16[1,16,16,128]{3,2,1,0:T(8,128)(2,1)S(1)}, u32[]{:S(2)}, u32[]{:S(2)}) collective-permute-start(bf16[1,16,16,128]{3,2,1,0:T(8,128)(2,1)} %slice.424), channel_id=1, source_target_pairs={{0,1020},{4,0},{8,4},{12,8},{16,12},{20,16},{24,20},{28,24},{32,28... | collective-permute-start | bytes 196616 | tf_op jit(solution)/shard_map/ppermute | solution.py:14
  21.5 4.3 %copy-start.13 = (bf16[1,729,32]{1,2,0:T(8,128)(2,1)S(1)}, bf16[1,729,32]{1,2,0:T(8,128)(2,1)}, u32[]{:S(2)}) copy-start(bf16[1,729,32]{1,2,0:T(8,128)(2,1)} %param.17) | copy-start | bytes 139972
  25.5 10.2 %copy-start.19 = (f32[2,2,2]{2,1,0:T(2,128)S(1)}, f32[2,2,2]{2,1,0:T(2,128)}, u32[]{:S(2)}) copy-start(f32[2,2,2]{2,1,0:T(2,128)} %param.14) | copy-start | bytes 100
  25.5 10.4 %copy-start.18 = (f32[16,256]{1,0:T(8,128)S(1)}, f32[16,256]{1,0:T(8,128)}, u32[]{:S(2)}) copy-start(f32[16,256]{1,0:T(8,128)} %param.13) | copy-start | bytes 49156
  26.7 15.1 %collective-permute-start.1 = (f32[1,32,128]{2,1,0:T(8,128)S(1)}, f32[1,32,128]{2,1,0:T(8,128)S(1)}, u32[]{:S(2)}, u32[]{:S(2)}) collective-permute-start(f32[1,32,128]{2,1,0:T(8,128)S(1)} %bitcast.216), channel_id=1, source_target_pairs={{0,1020},{4,0},{8,4},{12,8},{16,12},{20,16},{24,20},{28,24},{32,28... | collective-permute-start | bytes 49160 | tf_op jit(solution)/shard_map/ppermute | solution.py:14
  34.4 5.3 %copy-start.30 = (f32[1,32]{1,0:T(1,128)S(1)}, f32[1,32]{1,0:T(1,128)}, u32[]{:S(2)}) copy-start(f32[1,32]{1,0:T(1,128)} %param.18) | copy-start | bytes 388
  35.7 8.2 %copy-start.24 = (bf16[4]{0:T(256)(128)(2,1)}, bf16[4]{0:T(256)(128)(2,1)S(1)}, u32[]{:S(2)}) copy-start(bf16[4]{0:T(256)(128)(2,1)S(1)} %fusion.84) | copy-start | bytes 28
  35.8 9.3 %copy-start.22 = (f32[4]{0:T(128)}, f32[4]{0:T(128)S(1)}, u32[]{:S(2)}) copy-start(f32[4]{0:T(128)S(1)} %mul.172) | copy-start | bytes 52
  35.9 8.0 %copy-start.28 = (f32[4]{0:T(128)}, f32[4]{0:T(128)S(1)}, u32[]{:S(2)}) copy-start(f32[4]{0:T(128)S(1)} %mul.183) | copy-start | bytes 52
  39.7 5.4 %copy-start.26 = (bf16[4]{0:T(256)(128)(2,1)}, bf16[4]{0:T(256)(128)(2,1)S(1)}, u32[]{:S(2)}) copy-start(bf16[4]{0:T(256)(128)(2,1)S(1)} %fusion.82) | copy-start | bytes 28
  41.3 3.8 %copy-start.9 = (f32[4,128,729]{1,2,0:T(8,128)S(1)}, f32[4,128,729]{1,2,0:T(8,128)}, u32[]{:S(2)}) copy-start(f32[4,128,729]{1,2,0:T(8,128)} %fusion.14) | copy-start | bytes 4478980
  41.8 3.2 %collective-permute-start.2 = (bf16[1,32,128]{2,1,0:T(8,128)(2,1)S(1)}, bf16[1,32,128]{2,1,0:T(8,128)(2,1)S(1)}, u32[]{:S(2)}, u32[]{:S(2)}) collective-permute-start(bf16[1,32,128]{2,1,0:T(8,128)(2,1)S(1)} %multiply_convert_fusion.1), channel_id=1, source_target_pairs={{0,4},{4,8},{8,12},{12,16},{16,20},{20,24},{24,28},{28,32},{32,36}... | collective-permute-start | bytes 24584 | tf_op jit(solution)/shard_map/ppermute | solution.py:14
  57.3 9.9 %copy-start.3 = (f32[1,7,16,16,128]{4,0,3,2,1:T(1,128)}, f32[1,7,16,16,128]{4,0,3,2,1:T(1,128)S(1)}, u32[]{:S(2)}) copy-start(f32[1,7,16,16,128]{4,0,3,2,1:T(1,128)S(1)} %pad_maximum_fusion.6) | copy-start | bytes 2752516
  58.6 8.7 %copy-start.2 = (bf16[16,16,16,128]{3,2,1,0:T(8,128)(2,1)S(1)}, bf16[16,16,16,128]{3,2,1,0:T(8,128)(2,1)}, u32[]{:S(2)}) copy-start(bf16[16,16,16,128]{3,2,1,0:T(8,128)(2,1)} %param.11) | copy-start | bytes 3145732
  58.6 8.7 %copy-start.10 = (f32[16,16,16]{2,1,0:T(8,128)S(1)}, f32[16,16,16]{2,1,0:T(8,128)}, u32[]{:S(2)}) copy-start(f32[16,16,16]{2,1,0:T(8,128)} %mul.190) | copy-start | bytes 49156
  58.6 8.6 %collective-permute-start.3 = (f32[16,16,128]{2,1,0:T(8,128)S(1)}, f32[16,16,128]{2,1,0:T(8,128)S(1)}, u32[]{:S(2)}, u32[]{:S(2)}) collective-permute-start(f32[16,16,128]{2,1,0:T(8,128)S(1)} %bitcast.210), channel_id=1, source_target_pairs={{0,4},{4,8},{8,12},{12,16},{16,20},{20,24},{24,28},{28,32},{32,36}... | collective-permute-start | bytes 393224 | tf_op jit(solution)/shard_map/ppermute | solution.py:14
  84.9 11.1 %copy-start.7 = (bf16[16,16,16,128]{3,2,1,0:T(8,128)(2,1)S(1)}, bf16[16,16,16,128]{3,2,1,0:T(8,128)(2,1)}, u32[]{:S(2)}) copy-start(bf16[16,16,16,128]{3,2,1,0:T(8,128)(2,1)} %copy-done.6) | copy-start | bytes 3145732
  87.0 11.0 %collective-permute-start.4 = (bf16[1,16,16,128]{3,2,1,0:T(8,128)(2,1)S(1)}, bf16[1,16,16,128]{3,2,1,0:T(8,128)(2,1)S(1)}, u32[]{:S(2)}, u32[]{:S(2)}) collective-permute-start(bf16[1,16,16,128]{3,2,1,0:T(8,128)(2,1)S(1)} %copy-done.17), channel_id=1, source_target_pairs={{0,1020},{4,0},{8,4},{12,8},{16,12},{20,16},{24,20},{28,24},{32,28... | collective-permute-start | bytes 196616 | tf_op jit(solution)/shard_map/ppermute | solution.py:14
  96.1 16.0 %collective-permute-start.5 = (f32[1,32,128]{2,1,0:T(8,128)S(1)}, f32[1,32,128]{2,1,0:T(8,128)}, u32[]{:S(2)}, u32[]{:S(2)}) collective-permute-start(f32[1,32,128]{2,1,0:T(8,128)S(1)} %bitcast.217), channel_id=1, source_target_pairs={{0,1020},{4,0},{8,4},{12,8},{16,12},{20,16},{24,20},{28,24},{32,28... | collective-permute-start | bytes 49160 | tf_op jit(solution)/shard_map/ppermute | solution.py:14
  109.9 6.7 %copy-start.15 = (bf16[1,729,32]{1,2,0:T(8,128)(2,1)S(1)}, bf16[1,729,32]{1,2,0:T(8,128)(2,1)}, u32[]{:S(2)}) copy-start(bf16[1,729,32]{1,2,0:T(8,128)(2,1)} %param.16) | copy-start | bytes 139972
  109.9 6.7 %copy-start.25 = (bf16[4]{0:T(256)(128)(2,1)S(1)}, bf16[4]{0:T(256)(128)(2,1)}, u32[]{:S(2)}) copy-start(bf16[4]{0:T(256)(128)(2,1)} %copy-done.24) | copy-start | bytes 28
  109.9 6.7 %copy-start.29 = (f32[4]{0:T(128)S(1)}, f32[4]{0:T(128)}, u32[]{:S(2)}) copy-start(f32[4]{0:T(128)} %copy-done.28) | copy-start | bytes 52
  111.8 5.6 %copy-start.8 = (f32[4,128,729]{1,2,0:T(8,128)S(1)}, f32[4,128,729]{1,2,0:T(8,128)}, u32[]{:S(2)}) copy-start(f32[4,128,729]{1,2,0:T(8,128)} %fusion.10) | copy-start | bytes 4478980
  111.8 5.6 %copy-start.23 = (f32[4]{0:T(128)S(1)}, f32[4]{0:T(128)}, u32[]{:S(2)}) copy-start(f32[4]{0:T(128)} %copy-done.22) | copy-start | bytes 52
  111.8 5.6 %copy-start.27 = (bf16[4]{0:T(256)(128)(2,1)S(1)}, bf16[4]{0:T(256)(128)(2,1)}, u32[]{:S(2)}) copy-start(bf16[4]{0:T(256)(128)(2,1)} %copy-done.26) | copy-start | bytes 28
  113.0 4.4 %collective-permute-start.6 = (bf16[1,32,128]{2,1,0:T(8,128)(2,1)S(1)}, bf16[1,32,128]{2,1,0:T(8,128)(2,1)S(1)}, u32[]{:S(2)}, u32[]{:S(2)}) collective-permute-start(bf16[1,32,128]{2,1,0:T(8,128)(2,1)S(1)} %multiply_convert_fusion), channel_id=1, source_target_pairs={{0,4},{4,8},{8,12},{12,16},{16,20},{20,24},{24,28},{28,32},{32,36}... | collective-permute-start | bytes 24584 | tf_op jit(solution)/shard_map/ppermute | solution.py:14
  124.7 6.6 %collective-permute-start.7 = (f32[16,16,128]{2,1,0:T(8,128)S(1)}, f32[16,16,128]{2,1,0:T(8,128)S(1)}, u32[]{:S(2)}, u32[]{:S(2)}) collective-permute-start(f32[16,16,128]{2,1,0:T(8,128)S(1)} %get-tuple-element.18), channel_id=1, source_target_pairs={{0,4},{4,8},{8,12},{12,16},{16,20},{20,24},{24,28},{28,32},{32,36}... | collective-permute-start | bytes 393224 | tf_op jit(solution)/shard_map/ppermute | solution.py:14
  132.9 10.0 %copy-start.5 = (bf16[16,16,16,128]{3,2,1,0:T(8,128)(2,1)}, bf16[16,16,16,128]{3,2,1,0:T(8,128)(2,1)S(1)}, u32[]{:S(2)}) copy-start(bf16[16,16,16,128]{3,2,1,0:T(8,128)(2,1)S(1)} %fusion.5) | copy-start | bytes 3145732
  133.1 11.8 %collective-permute-start.8 = (bf16[1,16,16,128]{3,2,1,0:T(8,128)(2,1)S(1)}, bf16[1,16,16,128]{3,2,1,0:T(8,128)(2,1)S(1)}, u32[]{:S(2)}, u32[]{:S(2)}) collective-permute-start(bf16[1,16,16,128]{3,2,1,0:T(8,128)(2,1)S(1)} %slice.469), channel_id=1, source_target_pairs={{0,1020},{4,0},{8,4},{12,8},{16,12},{20,16},{24,20},{28,24},{32,28... | collective-permute-start | bytes 196616 | tf_op jit(solution)/shard_map/ppermute | solution.py:14
  142.9 5.1 %collective-permute-start.9 = (f32[1,32,128]{2,1,0:T(8,128)S(1)}, f32[1,32,128]{2,1,0:T(8,128)S(1)}, u32[]{:S(2)}, u32[]{:S(2)}) collective-permute-start(f32[1,32,128]{2,1,0:T(8,128)S(1)} %bitcast.218), channel_id=1, source_target_pairs={{0,1020},{4,0},{8,4},{12,8},{16,12},{20,16},{24,20},{28,24},{32,28... | collective-permute-start | bytes 49160 | tf_op jit(solution)/shard_map/ppermute | solution.py:14
  145.2 3.4 %copy-start.1 = (bf16[729,729]{1,0:T(8,128)(2,1)S(1)}, bf16[729,729]{1,0:T(8,128)(2,1)}, u32[]{:S(2)}) copy-start(bf16[729,729]{1,0:T(8,128)(2,1)} %param.15) | copy-start | bytes 3188650
  (9 other events, 15.5 us)
where the time goes:
time: 150 us; the launch traced here: 149 us
  starting transfers between devices  59 us (39%)
  local copies, waits for them, and re-layouts  46.1 us (31%)
  other arithmetic  19 us (13%)
  matrix products  11.7 us (8%)
  waiting for transfers between devices  8.96 us (6%)
  between operations  3.8 us (3%)
    ppermute x10, starting transfers between devices, shifted(): return lax.ppermute(value, axis, pairs)  59 us
    another operation x28, local copies, waits for them, and re-layouts, layer_blocks(): return jnp.stack(gathered)  19.2 us
    ppermute x10, waiting for transfers between devices, shifted(): return lax.ppermute(value, axis, pairs)  8.96 us
    unnamed x74, local copies, waits for them, and re-layouts  6.52 us
    concatenate x4, other arithmetic, wrap_sides(): return jnp.concatenate([planes, planes[:, :, :1]], axis=2)  5.59 us
    dot_general x2, matrix products, operator(): jnp.einsum('ij,ejb->eib', stiffness, bottom_blocks, preferred_element_typ...  4.93 us
    slice x2, local copies, waits for them, and re-layouts, assemble_blocks(): grouped[:, :, 0]  4.61 us
    concatenate x4, other arithmetic, join_pair(): return jnp.concatenate(pieces, axis=axis)  3.77 us
  transfers between devices with their start and end apart: 10, of which 5 were waited for; matrix products, arithmetic and copies ran while one was open for 20% of the time, Pallas kernels for 0%

commit v1 on v0

v1 whole, which is shorter than its diff:
```python
import functools

import jax
import jax.numpy as jnp
from jax import lax
from jax.experimental import pallas as pl
from jax.experimental.pallas import tpu as pltpu
from jax.sharding import PartitionSpec as P

MESH = pl.DeviceIdType.MESH
F32 = jnp.float32
BF16 = jnp.bfloat16

DEPTH = 768
MAIN = 576
FACE = 192
EDGE0 = 720
COEF0 = 736
NODES = 729
CH = 32


def node_selector():
    row = lax.broadcasted_iota(jnp.int32, (DEPTH, 128), 0)
    face = row - MAIN
    edge = row - EDGE0
    spot = jnp.bitwise_and(face, 15)
    old_main = (row >> 6) * 81 + jnp.bitwise_and(row >> 3, 7) * 9 + jnp.bitwise_and(row, 7)
    old_face = (face >> 4) * 81 + jnp.where(spot < 8, 72 + spot, (spot - 8) * 9 + 8)
    old_edge = jnp.where(edge < 9, edge * 81 + 80, -1)
    old = jnp.where(row < MAIN, old_main, jnp.where(row < EDGE0, old_face, old_edge))
    column = lax.broadcasted_iota(jnp.int32, (DEPTH, 128), 1)
    pieces = []
    for part in range(6):
        pieces.append((old == column + part * 128).astype(F32).astype(BF16))
    return jnp.concatenate(pieces, axis=1)[:, :NODES]


def dot(left, right):
    return jnp.dot(left, right, preferred_element_type=F32)


def kernel(
    wave_hbm, mass_hbm, pot_hbm, scale, stiff_hbm, lower_hbm, upper_hbm, kb, atom_col, count, upper_col,
    out_hbm, coef_out,
    wave, mass, pot, stiff, lower, upper, out_v,
    sel, kp, lp, lpt, up, upt, massb, potb, wv, wf, rim, zl, stepv,
    a_plane, a_held, b_rim, b_coef, send_plane, send_held, send_rim, send_coef,
    load_sem, store_sem, send_sem, recv_sem,
):
    me = lax.axis_index("space")
    n = lax.axis_size("space")
    right, left = lax.rem(me + 1, n), lax.rem(me + n - 1, n)

    loads = []
    for slot, (source, target) in enumerate(
        [(mass_hbm, mass), (wave_hbm, wave), (upper_hbm, upper), (stiff_hbm, stiff), (lower_hbm, lower), (pot_hbm, pot)]
    ):
        copy = pltpu.make_async_copy(source, target, load_sem.at[slot])
        copy.start()
        loads.append(copy)

    barrier = pltpu.get_barrier_semaphore()
    for neighbour in (left, right):
        pl.semaphore_signal(barrier, inc=1, device_id={"space": neighbour}, device_id_type=MESH)

    def remote(source, target, slot, neighbour):
        return pltpu.make_async_remote_copy(
            src_ref=source,
            dst_ref=target,
            send_sem=send_sem.at[slot],
            recv_sem=recv_sem.at[slot],
            device_id={"space": neighbour},
            device_id_type=MESH,
        )

    sel[...] = node_selector()
    for layer in range(2):
        for ab in range(4):
            rim[layer, ab, 160:192] = jnp.zeros((32, 128), BF16)

    def spread(source, target, planes):
        turned = jnp.transpose(source[...]).reshape(2, 8, 2, 8, 16)
        for p in planes:
            for a in range(2):
                for b in range(2):
                    block = turned[a, :, b, :, p : p + 1]
                    target[2 * a + b, p * 64 : p * 64 + 64] = jnp.broadcast_to(block, (8, 8, 128)).reshape(64, 128)

    def wave_block(p, a):
        both = wave[p, 8 * a : 8 * a + 8].astype(F32)
        return [both[:, 8 * b : 8 * b + 8].reshape(64, 128) for b in range(2)]

    def put_field(ab, p, value):
        rounded = value.astype(BF16)
        wv[ab, p * 64 : p * 64 + 64] = rounded
        wf[ab, p * 64 : p * 64 + 64] = rounded.astype(F32)

    def build_rim(layer):
        for a in range(2):
            for b in range(2):
                ab = 2 * a + b
                for i in range(9):
                    at = (8 * layer + i) * 64
                    j_face = wf[2 * (1 - a) + b, at : at + 8]
                    l_face = wf[2 * a + (1 - b), pl.ds(at, 8, stride=8)]
                    rim[layer, ab, i * 16 : i * 16 + 16] = jnp.concatenate([j_face, l_face], axis=0).astype(BF16)
                other = 2 * (1 - a) + (1 - b)
                edge = wf[other, pl.ds(8 * layer * 64, 8, stride=64)]
                last = wf[other, (8 * layer + 8) * 64 : (8 * layer + 8) * 64 + 8]
                rim[layer, ab, 144:160] = jnp.concatenate([edge, last], axis=0).astype(BF16)

    def bottom_operand(ab):
        return jnp.concatenate([wv[ab, 0:MAIN], rim[0, ab]], axis=0)

    def top_operand(ab, plane_slot):
        return jnp.concatenate([wv[ab, 512:1024], a_plane[plane_slot, ab], rim[1, ab]], axis=0)

    channel = lax.broadcasted_iota(jnp.int32, (CH, CH), 1)
    square = lax.broadcasted_iota(jnp.int32, (CH, CH), 0) == channel
    live = jnp.logical_and(square, channel < count[0])
    weight = jnp.sum(jnp.where(live, jnp.broadcast_to(kb[...], (CH, CH)), 0.0), axis=1, keepdims=True)

    loads[0].wait()
    spread(mass, massb, range(16))
    loads[1].wait()

    def start_field(planes):
        for p in planes:
            for a in range(2):
                for b, block in enumerate(wave_block(p, a)):
                    put_field(2 * a + b, p, massb[2 * a + b, p * 64 : p * 64 + 64] * block)

    start_field(range(0, 1))

    def send_plane_of(turn):
        for ab in range(4):
            send_plane[turn, ab] = wv[ab, 0:64]
        copy = remote(send_plane.at[turn], a_plane.at[turn], 4 * turn, left)
        copy.start()
        return copy

    def send_held_of(turn):
        send_held[turn] = dot(upt[...], bottom_operand(upper_col[0]))
        copy = remote(send_held.at[turn], a_held.at[turn], 4 * turn + 1, left)
        copy.start()
        return copy

    pl.semaphore_wait(barrier, 2)
    copies = [send_plane_of(0)]
    start_field(range(1, 9))
    build_rim(0)

    def turn_over(source, straight, across):
        picked = dot(sel[...], source[0])
        straight[...] = picked.astype(BF16)
        wide = jnp.concatenate([picked, jnp.zeros((DEPTH, 128 - CH), F32)], axis=1)
        across[...] = jnp.transpose(wide)[:CH].astype(BF16)

    loads[2].wait()
    turn_over(upper, up, upt)
    copies.append(send_held_of(0))
    start_field(range(9, 16))
    loads[3].wait()
    half = dot(sel[...], stiff[...]).astype(BF16)
    kp[...] = lax.dot_general(half, sel[...], (((1,), (1,)), ((), ())), preferred_element_type=F32).astype(BF16)
    loads[4].wait()
    turn_over(lower, lp, lpt)
    kp[:, COEF0:] = lp[...]
    loads[5].wait()
    spread(pot, potb, range(16))

    def layer_product(layer, rows, operands):
        for pair in range(2):
            both = jnp.concatenate(operands[2 * pair : 2 * pair + 2], axis=1)
            for low, high in rows:
                product = dot(kp[low:high], both)
                for k in range(2):
                    ab = 2 * pair + k
                    zl[layer, ab, low:high] = product[:, 128 * k : 128 * k + 128] * scale[layer, ab // 2, ab % 2]

    def bottom_product():
        layer_product(0, [(0, COEF0)], [bottom_operand(ab) for ab in range(4)])

    def add_rims(layer, planes):
        for i in planes:
            for a in range(2):
                for b in range(2):
                    ab = 2 * a + b
                    j_face = zl[layer, ab, MAIN + i * 16 : MAIN + i * 16 + 8]
                    l_face = zl[layer, ab, MAIN + i * 16 + 8 : MAIN + i * 16 + 16]
                    edge = zl[layer, ab, EDGE0 + i : EDGE0 + i + 1]
                    j_at = 2 * (1 - a) + b
                    l_at = 2 * a + (1 - b)
                    e_at = 2 * (1 - a) + (1 - b)
                    zl[layer, j_at, i * 64 : i * 64 + 8] = zl[layer, j_at, i * 64 : i * 64 + 8] + j_face
                    rows = pl.ds(i * 64, 8, stride=8)
                    zl[layer, l_at, rows] = zl[layer, l_at, rows] + l_face
                    zl[layer, e_at, i * 64 : i * 64 + 1] = zl[layer, e_at, i * 64 : i * 64 + 1] + edge

    def top_coef(turn, arrive):
        for ab in range(4):
            wf[ab, 1024:1088] = a_plane[turn, ab].astype(F32)
        build_rim(1)
        at = atom_col[0]
        own = dot(lpt[...], top_operand(at, turn))
        arrive.wait_recv()
        return own + a_held[turn]

    def elementwise(turn, planes):
        for p in planes:
            for a in range(2):
                waves = wave_block(p, a)
                filtered = []
                for b in range(2):
                    ab = 2 * a + b
                    rows = slice(p * 64, p * 64 + 64)
                    if p < 8:
                        total = zl[0, ab, p * 64 : p * 64 + 64]
                        if p == 0:
                            total = total + b_rim[turn, ab].astype(F32)
                    else:
                        total = zl[1, ab, (p - 8) * 64 : (p - 8) * 64 + 64]
                        if p == 8:
                            total = total + zl[0, ab, 512:576]
                    image = massb[ab, rows] * (total + potb[ab, rows] * wf[ab, rows])
                    if turn == 0:
                        step = ((image - waves[b]) * (1.0 / 6.0)).astype(BF16)
                        stepv[ab, rows] = step
                        put_field(ab, p, massb[ab, rows] * step.astype(F32))
                    else:
                        step = stepv[ab, rows].astype(F32)
                        value = (2.0 / 6.0) * (image - step) - waves[b]
                        put_field(ab, p, value)
                        filtered.append(value.reshape(8, 8, 128))
                if turn == 1:
                    out_v[p, 8 * a : 8 * a + 8] = jnp.concatenate(filtered, axis=1).astype(BF16)

    for turn in range(2):
        bottom_product()
        copies[-2].wait_recv()
        total = top_coef(turn, copies[-1]) * weight
        send_coef[turn] = total.astype(BF16)
        coef_copy = remote(send_coef.at[turn], b_coef.at[turn], 4 * turn + 2, right)
        coef_copy.start()
        for ab in range(4):
            inverse = jnp.full((CH, 128), 1.0, F32) / scale[1, ab // 2, ab % 2]
            inverse = jnp.where(atom_col[0] == ab, inverse, 0.0)
            rim[1, ab, 160:192] = (total * inverse).astype(BF16)
        operands = [top_operand(ab, turn) for ab in range(4)]
        layer_product(1, [(512, 576), (704, COEF0)], operands)
        add_rims(1, range(8, 9))
        for ab in range(4):
            send_rim[turn, ab] = zl[1, ab, 512:576].astype(BF16)
        rim_copy = remote(send_rim.at[turn], b_rim.at[turn], 4 * turn + 3, right)
        rim_copy.start()
        layer_product(1, [(0, 512), (MAIN, 704)], operands)
        add_rims(1, range(0, 8))
        elementwise(turn, range(9, 16))
        if turn == 1:
            early = pltpu.make_async_copy(out_v.at[9:16], out_hbm.at[9:16], store_sem.at[0])
            early.start()
        coef_copy.wait_recv()
        spread_coef = dot(up[:COEF0], b_coef[turn])
        for ab in range(4):
            chosen = jnp.where(upper_col[0] == ab, 1.0, 0.0)
            zl[0, ab, 0:COEF0] = zl[0, ab, 0:COEF0] + spread_coef * chosen
        add_rims(0, range(9))
        rim_copy.wait_recv()
        elementwise(turn, range(0, 9))
        build_rim(0)
        copies.append(coef_copy)
        copies.append(rim_copy)
        copies.append(send_plane_of(turn + 1))
        copies.append(send_held_of(turn + 1))

    late = pltpu.make_async_copy(out_v.at[0:9], out_hbm.at[0:9], store_sem.at[1])
    late.start()
    copies[-2].wait_recv()
    coef_out[0] = top_coef(2, copies[-1])
    for copy in copies:
        copy.wait_send()
    early.wait()
    late.wait()


def per_device(*arrays):
    wave_in = arrays[0]
    any_space = pl.BlockSpec(memory_space=pl.ANY)
    vmem = pl.BlockSpec(memory_space=pltpu.VMEM)
    smem = pl.BlockSpec(memory_space=pltpu.SMEM)
    return pl.pallas_call(
        kernel,
        out_shape=(
            jax.ShapeDtypeStruct(wave_in.shape, BF16),
            jax.ShapeDtypeStruct((1, CH, 128), F32),
        ),
        in_specs=[any_space, any_space, any_space, smem, any_space, any_space, any_space, vmem, smem, smem, smem],
        out_specs=(any_space, vmem),
        scratch_shapes=[
            pltpu.VMEM((16, 16, 16, 128), BF16),
            pltpu.VMEM((16, 256), F32),
            pltpu.VMEM((16, 256), F32),
            pltpu.VMEM((NODES, NODES), BF16),
            pltpu.VMEM((1, NODES, CH), BF16),
            pltpu.VMEM((1, NODES, CH), BF16),
            pltpu.VMEM((16, 16, 16, 128), BF16),
            pltpu.VMEM((DEPTH, NODES), BF16),
            pltpu.VMEM((DEPTH, DEPTH), BF16),
            pltpu.VMEM((DEPTH, CH), BF16),
            pltpu.VMEM((CH, DEPTH), BF16),
            pltpu.VMEM((DEPTH, CH), BF16),
            pltpu.VMEM((CH, DEPTH), BF16),
            pltpu.VMEM((4, 1024, 128), F32),
            pltpu.VMEM((4, 1024, 128), F32),
            pltpu.VMEM((4, 1024, 128), BF16),
            pltpu.VMEM((4, 1088, 128), F32),
            pltpu.VMEM((2, 4, FACE, 128), BF16),
            pltpu.VMEM((2, 4, COEF0, 128), F32),
            pltpu.VMEM((4, 1024, 128), BF16),
            pltpu.VMEM((3, 4, 64, 128), BF16),
            pltpu.VMEM((3, CH, 128), F32),
            pltpu.VMEM((2, 4, 64, 128), BF16),
            pltpu.VMEM((2, CH, 128), BF16),
            pltpu.VMEM((3, 4, 64, 128), BF16),
            pltpu.VMEM((3, CH, 128), F32),
            pltpu.VMEM((2, 4, 64, 128), BF16),
            pltpu.VMEM((2, CH, 128), BF16),
            pltpu.SemaphoreType.DMA((6,)),
            pltpu.SemaphoreType.DMA((2,)),
            pltpu.SemaphoreType.DMA((10,)),
            pltpu.SemaphoreType.DMA((10,)),
        ],
        compiler_params=pltpu.CompilerParams(
            collective_id=0, has_side_effects=True, vmem_limit_bytes=48 * 1024 * 1024
        ),
    )(*arrays)


def solution(mesh):
    in_specs = (
        P("space", None, None, "band"),
        P("space", None),
        P("space", None),
        P("space", None, None),
        P(),
        P("space", None, None),
        P("space", None, None),
        P("space", None),
        P("space"),
        P("space"),
        P("space"),
    )
    out_specs = (P("space", None, None, "band"), P("space", None, "band"))
    return jax.shard_map(
        per_device, mesh=mesh, in_specs=in_specs, out_specs=out_specs, check_vma=False
    )
```

time: 150 us -> 55.4 us (0.37)
  the two profiles are of different devices: /device:TPU:1 before, /device:TPU:16 now
where the time goes in v1:
time: 55.4 us; the launch traced here: 54.9 us
  Pallas kernels  43.6 us (79%)
  local copies, waits for them, and re-layouts  8.75 us (16%)
  between operations  2.59 us (5%)
    pallas_call x1, Pallas kernels, per_device(): pl.pallas_call(kernel, out_shape=(jax.ShapeDtypeStruct(wave_in.shape, BF1...  43.6 us
    unnamed x16, local copies, waits for them, and re-layouts  8.75 us

profile of v1, /device:TPU:16, one launch (start us, length us, event | category | flops | bytes accessed | tf_op | source)
XLA Modules:
  0.0 54.9 jit_solution(8991303204179229891)
XLA Ops:
  2.6 1.0 %copy.13.lower_hbm = bf16[1,729,32]{2,1,0:T(8,128)(2,1)S(1)} copy(bf16[1,729,32]{1,2,0:T(8,128)(2,1)} %param.16) | data formatting | bytes 93312 | tf_op args[5]
  3.5 1.0 %copy.14.upper_hbm = bf16[1,729,32]{2,1,0:T(8,128)(2,1)S(1)} copy(bf16[1,729,32]{1,2,0:T(8,128)(2,1)} %param.17) | data formatting | bytes 93312 | tf_op args[6]
  4.5 0.0 copy-start
  4.5 1.3 %copy-done = bf16[729,729]{1,0:T(8,128)(2,1)S(1)} copy-done((bf16[729,729]{1,0:T(8,128)(2,1)S(1)}, bf16[729,729]{1,0:T(8,128)(2,1)}, u32[]{:S(2)}) %copy-start) | copy-done | bytes 1062906
  5.8 0.0 copy-start.1
  5.8 1.2 %copy-done.1 = bf16[16,16,16,128]{3,2,1,0:T(8,128)(2,1)S(1)} copy-done((bf16[16,16,16,128]{3,2,1,0:T(8,128)(2,1)S(1)}, bf16[16,16,16,128]{3,2,1,0:T(8,128)(2,1)}, u32[]{:S(2)}) %copy-start.1) | copy-done | bytes 1048600
  7.0 0.0 copy-start.2
  7.0 0.7 %copy-done.2 = f32[16,256]{1,0:T(8,128)S(1)} copy-done((f32[16,256]{1,0:T(8,128)S(1)}, f32[16,256]{1,0:T(8,128)}, u32[]{:S(2)}) %copy-start.2) | copy-done | bytes 16408
  7.7 0.0 copy-start.3
  7.7 0.7 %copy-done.3 = f32[16,256]{1,0:T(8,128)S(1)} copy-done((f32[16,256]{1,0:T(8,128)S(1)}, f32[16,256]{1,0:T(8,128)}, u32[]{:S(2)}) %copy-start.3) | copy-done | bytes 16408
  8.4 0.0 copy-start.4
  8.4 0.7 %copy-done.4 = f32[2,2,2]{2,1,0:T(2,128)S(1)} copy-done((f32[2,2,2]{2,1,0:T(2,128)S(1)}, f32[2,2,2]{2,1,0:T(2,128)}, u32[]{:S(2)}) %copy-start.4) | copy-done | bytes 56
  9.1 0.0 copy-start.5
  9.1 0.7 %copy-done.5 = f32[1,32]{1,0:T(1,128)S(1)} copy-done((f32[1,32]{1,0:T(1,128)S(1)}, f32[1,32]{1,0:T(1,128)}, u32[]{:S(2)}) %copy-start.5) | copy-done | bytes 152
  9.8 43.6 %shard_map.122 = (bf16[16,16,16,128]{3,2,1,0:T(8,128)(2,1)S(1)}, f32[1,32,128]{2,1,0:T(8,128)S(1)}) custom-call(bf16[16,16,16,128]{3,2,1,0:T(8,128)(2,1)S(1)} %copy-done.1, f32[16,256]{1,0:T(8,128)S(1)} %copy-done.2, f32[16,256]{1,0:T(8,128)S(1)} %copy-done.3, f32[2,2,2]{2,1,0:T(2,128)S(1)} %copy-done.4, bf16[729,729]{1,0:T(8,128)(2,1)S(1)} %copy-done, ...), custom_call_target="tpu_custom_call" | custom-call | tf_op jit(solution)/shard_map/pallas_call | solution.py:292
  53.4 1.0 %copy.20 = bf16[16,16,16,128]{3,2,1,0:T(8,128)(2,1)} copy(bf16[16,16,16,128]{3,2,1,0:T(8,128)(2,1)S(1)} %get-tuple-element.4) | data formatting | bytes 2097152
  54.3 0.6 %copy.21 = f32[1,32,128]{2,1,0:T(8,128)} copy(f32[1,32,128]{2,1,0:T(8,128)S(1)} %get-tuple-element.5) | data formatting | bytes 32768
Async XLA Ops:
  4.5 1.3 %copy-start = (bf16[729,729]{1,0:T(8,128)(2,1)S(1)}, bf16[729,729]{1,0:T(8,128)(2,1)}, u32[]{:S(2)}) copy-start(bf16[729,729]{1,0:T(8,128)(2,1)} %stiff_hbm.1) | copy-start | bytes 3188650
  5.8 1.2 %copy-start.1 = (bf16[16,16,16,128]{3,2,1,0:T(8,128)(2,1)S(1)}, bf16[16,16,16,128]{3,2,1,0:T(8,128)(2,1)}, u32[]{:S(2)}) copy-start(bf16[16,16,16,128]{3,2,1,0:T(8,128)(2,1)} %wave_hbm.1) | copy-start | bytes 3145732
  7.0 0.7 %copy-start.2 = (f32[16,256]{1,0:T(8,128)S(1)}, f32[16,256]{1,0:T(8,128)}, u32[]{:S(2)}) copy-start(f32[16,256]{1,0:T(8,128)} %mass_hbm.1) | copy-start | bytes 49156
  7.7 0.7 %copy-start.3 = (f32[16,256]{1,0:T(8,128)S(1)}, f32[16,256]{1,0:T(8,128)}, u32[]{:S(2)}) copy-start(f32[16,256]{1,0:T(8,128)} %pot_hbm.1) | copy-start | bytes 49156
  8.4 0.7 %copy-start.4 = (f32[2,2,2]{2,1,0:T(2,128)S(1)}, f32[2,2,2]{2,1,0:T(2,128)}, u32[]{:S(2)}) copy-start(f32[2,2,2]{2,1,0:T(2,128)} %scale.1) | copy-start | bytes 100
  9.1 0.7 %copy-start.5 = (f32[1,32]{1,0:T(1,128)S(1)}, f32[1,32]{1,0:T(1,128)}, u32[]{:S(2)}) copy-start(f32[1,32]{1,0:T(1,128)} %kb.1) | copy-start | bytes 388

commit v2 on v1

v2 whole, which is shorter than its diff:
```python
import functools

import jax
import jax.numpy as jnp
from jax import lax
from jax.experimental import pallas as pl
from jax.experimental.pallas import tpu as pltpu
from jax.sharding import PartitionSpec as P

MESH = pl.DeviceIdType.MESH
F32 = jnp.float32
BF16 = jnp.bfloat16

DEPTH = 768
MAIN = 576
FACE = 192
EDGE0 = 720
COEF0 = 736
NODES = 729
CH = 32


def node_selector():
    row = lax.broadcasted_iota(jnp.int32, (DEPTH, 128), 0)
    face = row - MAIN
    edge = row - EDGE0
    spot = jnp.bitwise_and(face, 15)
    old_main = (row >> 6) * 81 + jnp.bitwise_and(row >> 3, 7) * 9 + jnp.bitwise_and(row, 7)
    old_face = (face >> 4) * 81 + jnp.where(spot < 8, 72 + spot, (spot - 8) * 9 + 8)
    old_edge = jnp.where(edge < 9, edge * 81 + 80, -1)
    old = jnp.where(row < MAIN, old_main, jnp.where(row < EDGE0, old_face, old_edge))
    column = lax.broadcasted_iota(jnp.int32, (DEPTH, 128), 1)
    pieces = []
    for part in range(6):
        pieces.append((old == column + part * 128).astype(F32).astype(BF16))
    return jnp.concatenate(pieces, axis=1)[:, :NODES]


def dot(left, right):
    return jnp.dot(left, right, preferred_element_type=F32)


def dot_turned(left, right):
    return lax.dot_general(left, right, (((1,), (1,)), ((), ())), preferred_element_type=F32)


def kernel(
    wave_hbm, mass_hbm, pot_hbm, scale_hbm, stiff_hbm, lower_hbm, upper_hbm, kb_hbm, atom_col, count, upper_col,
    out_hbm, coef_hbm,
    wave, mass, pot, stiff, lower, upper, scale, kb, out_v, coef_v,
    sel, kp, both, both_t, massb, potb, mrim, wv, wf, rim, zl, stepv, pf, plane16, mass16, ez, e0,
    a_plane, a_held, a_edge, a_mass, a_gram, b_rim, b_coef,
    send_plane, send_held, send_edge, send_gram, send_rim, send_coef,
    load_sem, store_sem, send_sem, recv_sem,
):
    me = lax.axis_index("space")
    n = lax.axis_size("space")
    right, left = lax.rem(me + 1, n), lax.rem(me + n - 1, n)
    share = (1.0 / 6.0, 2.0 / 6.0)

    barrier = pltpu.get_barrier_semaphore()
    for neighbour in (left, right):
        pl.semaphore_signal(barrier, inc=1, device_id={"space": neighbour}, device_id_type=MESH)

    loads = []
    for slot, (source, target) in enumerate(
        [
            (mass_hbm, mass),
            (wave_hbm, wave),
            (upper_hbm, upper),
            (lower_hbm, lower),
            (stiff_hbm, stiff),
            (pot_hbm, pot),
            (scale_hbm, scale),
            (kb_hbm, kb),
        ]
    ):
        copy = pltpu.make_async_copy(source, target, load_sem.at[slot])
        copy.start()
        loads.append(copy)

    copies = []

    def remote(source, target, slot, neighbour):
        copy = pltpu.make_async_remote_copy(
            src_ref=source,
            dst_ref=target,
            send_sem=send_sem.at[slot],
            recv_sem=recv_sem.at[slot],
            device_id={"space": neighbour},
            device_id_type=MESH,
        )
        copy.start()
        copies.append(copy)
        return copy

    sel[...] = node_selector()
    for layer in range(2):
        for ab in range(4):
            rim[layer, ab, 160:192] = jnp.zeros((32, 128), BF16)

    def spread(turned, target, planes):
        turned = turned.reshape(2, 8, 2, 8, turned.shape[-1])
        for p in planes:
            for a in range(2):
                for b in range(2):
                    block = turned[a, :, b, :, p : p + 1]
                    target[2 * a + b, p * 64 : p * 64 + 64] = jnp.broadcast_to(block, (8, 8, 128)).reshape(64, 128)

    def wave_block(p, a):
        both_b = wave[p, 8 * a : 8 * a + 8].astype(F32)
        return [both_b[:, 8 * b : 8 * b + 8].reshape(64, 128) for b in range(2)]

    def put_field(ab, p, value):
        rounded = value.astype(BF16)
        wv[ab, p * 64 : p * 64 + 64] = rounded
        wf[ab, p * 64 : p * 64 + 64] = rounded.astype(F32)

    def gather_rim(source, base, put):
        for a in range(2):
            for b in range(2):
                ab = 2 * a + b
                for i in range(9):
                    at = base + i * 64
                    j_face = source[2 * (1 - a) + b, at : at + 8]
                    l_face = source[2 * a + (1 - b), pl.ds(at, 8, stride=8)]
                    put(ab, i * 16, jnp.concatenate([j_face, l_face], axis=0))
                other = 2 * (1 - a) + (1 - b)
                edge = source[other, pl.ds(base, 8, stride=64)]
                last = source[other, base + 512 : base + 520]
                put(ab, 144, jnp.concatenate([edge, last], axis=0))

    def build_rim(layer):
        def put(ab, row, value):
            rim[layer, ab, row : row + 16] = value.astype(BF16)

        gather_rim(wf, 512 * layer, put)

    def bottom_operand(ab):
        return jnp.concatenate([wv[ab, 0:MAIN], rim[0, ab]], axis=0)

    def top_operand(ab):
        return jnp.concatenate([wv[ab, 512:1024], plane16[ab], rim[1, ab]], axis=0)

    loads[0].wait()
    spread(jnp.transpose(mass[...]), massb, range(16))
    loads[1].wait()

    def start_field(planes):
        for p in planes:
            for a in range(2):
                for b, block in enumerate(wave_block(p, a)):
                    put_field(2 * a + b, p, massb[2 * a + b, p * 64 : p * 64 + 64] * block)

    def send_held_of(turn):
        send_held[turn] = dot(both_t[0:CH], bottom_operand(upper_col[0]))
        return remote(send_held.at[turn], a_held.at[turn], 3 + turn, left)

    start_field(range(0, 1))
    for ab in range(4):
        send_plane[0, ab] = wv[ab, 0:64]
    pl.semaphore_wait(barrier, 2)
    plane_copy = remote(send_plane.at[0], a_plane.at[0], 0, left)
    loads[2].wait()
    loads[3].wait()
    turned = dot_turned(jnp.concatenate([upper[0], lower[0]], axis=0), sel[...])
    both_t[...] = turned.astype(BF16)
    start_field(range(1, 9))
    build_rim(0)
    held_copy = send_held_of(0)
    both[...] = jnp.transpose(jnp.concatenate([turned, jnp.zeros((64, DEPTH), F32)], axis=0)).astype(BF16)
    loads[4].wait()
    half = dot(sel[...], stiff[...]).astype(BF16)
    kp[...] = dot_turned(half, sel[...]).astype(BF16)
    kp[:, COEF0:] = both[:, CH : 2 * CH]
    start_field(range(9, 16))
    for slot in (5, 6, 7):
        loads[slot].wait()
    spread(jnp.transpose(pot[...]), potb, range(16))

    channel = lax.broadcasted_iota(jnp.int32, (CH, CH), 1)
    square = lax.broadcasted_iota(jnp.int32, (CH, CH), 0) == channel
    live = jnp.logical_and(square, channel < count[0])
    weight = jnp.sum(jnp.where(live, jnp.broadcast_to(kb[...], (CH, CH)), 0.0), axis=1, keepdims=True)

    def scale_of(layer, ab, rows):
        return jnp.broadcast_to(scale[layer, ab // 2 : ab // 2 + 1, ab % 2 : ab % 2 + 1], (rows, 128))

    def chosen(column, ab):
        return jnp.where(column[0] == ab, 1.0, 0.0)

    def layer_product(layer, rows, operands):
        for pair in range(2):
            wide = jnp.concatenate(operands[2 * pair : 2 * pair + 2], axis=1)
            for low, high in rows:
                product = dot(kp[low:high], wide)
                for k in range(2):
                    ab = 2 * pair + k
                    zl[layer, ab, low:high] = product[:, 128 * k : 128 * k + 128] * scale_of(layer, ab, high - low)

    def add_rims(target, planes, face, edge_row):
        for i in planes:
            for a in range(2):
                for b in range(2):
                    ab = 2 * a + b
                    j_at, l_at, e_at = 2 * (1 - a) + b, 2 * a + (1 - b), 2 * (1 - a) + (1 - b)
                    j_face = target[ab, face + i * 16 : face + i * 16 + 8]
                    l_face = target[ab, face + i * 16 + 8 : face + i * 16 + 16]
                    edge = target[ab, edge_row + i : edge_row + i + 1]
                    target[j_at, i * 64 : i * 64 + 8] = target[j_at, i * 64 : i * 64 + 8] + j_face
                    rows = pl.ds(i * 64, 8, stride=8)
                    target[l_at, rows] = target[l_at, rows] + l_face
                    target[e_at, i * 64 : i * 64 + 1] = target[e_at, i * 64 : i * 64 + 1] + edge

    def layer_rims(layer, planes):
        add_rims(zl.at[layer], planes, MAIN, EDGE0)

    def set_up():
        for ab in range(4):
            part = chosen(upper_col, ab)
            ez[ab, 0:64] = both[0:64].astype(F32) * part
            ez[ab, 64:80] = both[MAIN : MAIN + 16].astype(F32) * part
            ez[ab, 80:96] = both[EDGE0 : EDGE0 + 16].astype(F32) * part
        add_rims(ez, range(1), 64, 80)
        placed = jnp.transpose(jnp.concatenate([ez[ab, 0:64] for ab in range(4)], axis=0))
        send_edge[...] = placed[0:CH].astype(BF16)
        sent = [remote(send_edge, a_edge, 6, left), remote(mass.at[0:8], a_mass, 7, left)]

        def put(ab, row, value):
            mrim[ab, row : row + 16] = value

        for ab in range(4):
            mrim[ab, 160:192] = jnp.zeros((32, 128), F32)
        gather_rim(massb, 0, put)
        at = upper_col[0]
        node_mass = jnp.concatenate([massb[at, 0:MAIN], mrim[at]], axis=0)
        wide = both[...].astype(F32) * node_mass
        send_gram[0] = dot(both_t[0:CH], (wide * node_mass).astype(BF16)) * share[0]
        send_gram[1] = dot(both_t[0:CH], wide.astype(BF16)) * share[1]
        sent.append(remote(send_gram, a_gram, 8, left))
        return sent

    def take_set_up(sent):
        sent[0].wait_recv()
        sent[1].wait_recv()
        wide = jnp.concatenate([a_edge[...].astype(F32), jnp.zeros((128 - CH, 256), F32)], axis=0)
        e0[...] = jnp.transpose(wide)[:, 0:CH].astype(BF16)
        spread(jnp.transpose(a_mass[...]), mass16, range(1))

    def finish_plane(turn):
        before = turn - 1
        coef = send_coef[before]
        placed = dot(e0[...], coef)
        shares = []
        parts = []
        for ab in range(4):
            edge_sum = send_rim[before, ab].astype(F32)
            amount = mass16[ab] * share[before]
            parts.append(amount * (edge_sum + placed[64 * ab : 64 * ab + 64]))
            shares.append((amount * edge_sum * mass16[ab] if turn == 1 else amount * edge_sum).astype(BF16))
        held = dot(a_edge[...], jnp.concatenate(shares, axis=0))
        held = held + jnp.dot(
            a_gram[before, :, 0:CH], coef.astype(F32), preferred_element_type=F32, precision=lax.Precision.HIGHEST
        )
        return parts, held

    def top_coef(turn, plane_copy, held_copy, setting):
        if turn > 0:
            if turn == 1:
                take_set_up(setting)
                setting[2].wait_recv()
            parts, extra = finish_plane(turn)
        plane_copy.wait_recv()
        for ab in range(4):
            value = a_plane[turn, ab].astype(F32)
            if turn > 0:
                value = value + parts[ab]
            if turn == 1:
                value = mass16[ab] * value.astype(BF16).astype(F32)
            value = value.astype(BF16)
            plane16[ab] = value
            wf[ab, 1024:1088] = value.astype(F32)
        build_rim(1)
        own = dot(both_t[CH : 2 * CH], top_operand(atom_col[0]))
        held_copy.wait_recv()
        own = own + a_held[turn]
        return own if turn == 0 else own + extra

    def combine(turn, p, ab, total, wave_part):
        rows = slice(p * 64, p * 64 + 64)
        image = massb[ab, rows] * (total + potb[ab, rows] * wf[ab, rows])
        if turn == 0:
            return (image - wave_part) * share[0]
        return share[1] * (image - stepv[ab, rows].astype(F32)) - wave_part

    def keep(turn, p, a, values):
        if turn == 0:
            for b in range(2):
                ab = 2 * a + b
                step = values[b].astype(BF16)
                stepv[ab, p * 64 : p * 64 + 64] = step
                put_field(ab, p, massb[ab, p * 64 : p * 64 + 64] * step.astype(F32))
            return
        if p >= 8:
            for b in range(2):
                put_field(2 * a + b, p, values[b])
        pieces = [value.reshape(8, 8, 128) for value in values]
        out_v[p, 8 * a : 8 * a + 8] = jnp.concatenate(pieces, axis=1).astype(BF16)

    def top_planes(turn):
        for p in range(9, 16):
            for a in range(2):
                waves = wave_block(p, a)
                values = []
                for b in range(2):
                    ab = 2 * a + b
                    total = zl[1, ab, (p - 8) * 64 : (p - 8) * 64 + 64]
                    values.append(combine(turn, p, ab, total, waves[b]))
                keep(turn, p, a, values)

    def bottom_planes_partly(turn):
        for p in range(9):
            for a in range(2):
                waves = wave_block(p, a)
                for b in range(2):
                    ab = 2 * a + b
                    rows = slice(p * 64, p * 64 + 64)
                    total = zl[0, ab, rows]
                    if p == 8:
                        total = total + zl[1, ab, 0:64]
                    value = combine(turn, p, ab, total, waves[b])
                    pf[ab, rows] = value
                    if p == 0:
                        send_plane[turn + 1, ab] = value.astype(BF16)
                    put_field(ab, p, massb[ab, rows] * value if turn == 0 else value)

    def bottom_planes(turn):
        for p in range(9):
            for a in range(2):
                values = []
                for b in range(2):
                    ab = 2 * a + b
                    rows = slice(p * 64, p * 64 + 64)
                    extra = zl[0, ab, rows]
                    if p == 0:
                        extra = extra + b_rim[turn, ab].astype(F32)
                    values.append(pf[ab, rows] + massb[ab, rows] * share[turn] * extra)
                keep(turn, p, a, values)

    for turn in range(2):
        layer_product(0, [(0, COEF0)], [bottom_operand(ab) for ab in range(4)])
        layer_rims(0, range(9))
        if turn == 0:
            setting = set_up()
        total = top_coef(turn, plane_copy, held_copy, setting) * weight
        send_coef[turn] = total.astype(BF16)
        coef_copy = remote(send_coef.at[turn], b_coef.at[turn], 9 + turn, right)
        for ab in range(4):
            part = (total / scale_of(1, ab, CH)) * chosen(atom_col, ab)
            rim[1, ab, 160:192] = part.astype(BF16)
        operands = [top_operand(ab) for ab in range(4)]
        layer_product(1, [(512, 576), (704, COEF0)], operands)
        layer_rims(1, range(8, 9))
        for ab in range(4):
            send_rim[turn, ab] = zl[1, ab, 512:576].astype(BF16)
        rim_copy = remote(send_rim.at[turn], b_rim.at[turn], 11 + turn, right)
        layer_product(1, [(0, 512), (MAIN, 704)], operands)
        layer_rims(1, range(0, 8))
        bottom_planes_partly(turn)
        plane_copy = remote(send_plane.at[turn + 1], a_plane.at[turn + 1], turn + 1, left)
        build_rim(0)
        held_copy = send_held_of(turn + 1)
        top_planes(turn)
        if turn == 1:
            early = pltpu.make_async_copy(out_v.at[9:16], out_hbm.at[9:16], store_sem.at[0])
            early.start()
        coef_copy.wait_recv()
        spread_coef = dot(both[:COEF0, 0:CH], b_coef[turn])
        for ab in range(4):
            zl[0, ab, 0:COEF0] = spread_coef * chosen(upper_col, ab)
        layer_rims(0, range(9))
        rim_copy.wait_recv()
        bottom_planes(turn)
        if turn == 0:
            build_rim(0)

    late = pltpu.make_async_copy(out_v.at[0:9], out_hbm.at[0:9], store_sem.at[1])
    late.start()
    coef_v[0] = top_coef(2, plane_copy, held_copy, setting)
    last = pltpu.make_async_copy(coef_v, coef_hbm, store_sem.at[2])
    last.start()
    for copy in copies:
        copy.wait_send()
    early.wait()
    late.wait()
    last.wait()


def per_device(*arrays):
    arrays = list(arrays)
    wave_in = arrays[0]
    arrays[5] = jnp.swapaxes(arrays[5], 1, 2)
    arrays[6] = jnp.swapaxes(arrays[6], 1, 2)
    any_space = pl.BlockSpec(memory_space=pl.ANY)
    smem = pl.BlockSpec(memory_space=pltpu.SMEM)
    return pl.pallas_call(
        kernel,
        out_shape=(
            jax.ShapeDtypeStruct(wave_in.shape, BF16),
            jax.ShapeDtypeStruct((1, CH, 128), F32),
        ),
        in_specs=[any_space] * 8 + [smem] * 3,
        out_specs=(any_space, any_space),
        scratch_shapes=[
            pltpu.VMEM((16, 16, 16, 128), BF16),
            pltpu.VMEM((16, 256), F32),
            pltpu.VMEM((16, 256), F32),
            pltpu.VMEM((NODES, NODES), BF16),
            pltpu.VMEM((1, CH, NODES), BF16),
            pltpu.VMEM((1, CH, NODES), BF16),
            pltpu.VMEM((2, 2, 2), F32),
            pltpu.VMEM((1, CH), F32),
            pltpu.VMEM((16, 16, 16, 128), BF16),
            pltpu.VMEM((1, CH, 128), F32),
            pltpu.VMEM((DEPTH, NODES), BF16),
            pltpu.VMEM((DEPTH, DEPTH), BF16),
            pltpu.VMEM((DEPTH, 128), BF16),
            pltpu.VMEM((2 * CH, DEPTH), BF16),
            pltpu.VMEM((4, 1024, 128), F32),
            pltpu.VMEM((4, 1024, 128), F32),
            pltpu.VMEM((4, FACE, 128), F32),
            pltpu.VMEM((4, 1024, 128), BF16),
            pltpu.VMEM((4, 1088, 128), F32),
            pltpu.VMEM((2, 4, FACE, 128), BF16),
            pltpu.VMEM((2, 4, COEF0, 128), F32),
            pltpu.VMEM((4, 1024, 128), BF16),
            pltpu.VMEM((4, MAIN, 128), F32),
            pltpu.VMEM((4, 64, 128), BF16),
            pltpu.VMEM((4, 64, 128), F32),
            pltpu.VMEM((4, 96, 128), F32),
            pltpu.VMEM((256, CH), BF16),
            pltpu.VMEM((3, 4, 64, 128), BF16),
            pltpu.VMEM((3, CH, 128), F32),
            pltpu.VMEM((CH, 256), BF16),
            pltpu.VMEM((8, 256), F32),
            pltpu.VMEM((2, CH, 128), F32),
            pltpu.VMEM((2, 4, 64, 128), BF16),
            pltpu.VMEM((2, CH, 128), BF16),
            pltpu.VMEM((3, 4, 64, 128), BF16),
            pltpu.VMEM((3, CH, 128), F32),
            pltpu.VMEM((CH, 256), BF16),
            pltpu.VMEM((2, CH, 128), F32),
            pltpu.VMEM((2, 4, 64, 128), BF16),
            pltpu.VMEM((2, CH, 128), BF16),
            pltpu.SemaphoreType.DMA((8,)),
            pltpu.SemaphoreType.DMA((3,)),
            pltpu.SemaphoreType.DMA((13,)),
            pltpu.SemaphoreType.DMA((13,)),
        ],
        compiler_params=pltpu.CompilerParams(
            collective_id=0, has_side_effects=True, vmem_limit_bytes=63 * 1024 * 1024
        ),
    )(*arrays)


def solution(mesh):
    in_specs = (
        P("space", None, None, "band"),
        P("space", None),
        P("space", None),
        P("space", None, None),
        P(),
        P("space", None, None),
        P("space", None, None),
        P("space", None),
        P("space"),
        P("space"),
        P("space"),
    )
    out_specs = (P("space", None, None, "band"), P("space", None, "band"))
    return jax.shard_map(
        per_device, mesh=mesh, in_specs=in_specs, out_specs=out_specs, check_vma=False
    )
```

time: 55.4 us -> 42.1 us (0.76)
  the two profiles are of different devices: /device:TPU:16 before, /device:TPU:8 now
where the time goes in v2:
time: 42.1 us; the launch traced here: 41.9 us
  Pallas kernels  36.3 us (86%)
  local copies, waits for them, and re-layouts  3.04 us (7%)
  between operations  2.59 us (6%)
    pallas_call x1, Pallas kernels, per_device(): pl.pallas_call(kernel, out_shape=(jax.ShapeDtypeStruct(wave_in.shape, BF1...  36.3 us
    unnamed x4, local copies, waits for them, and re-layouts  3.04 us

profile of v2, /device:TPU:8, one launch (start us, length us, event | category | flops | bytes accessed | tf_op | source)
XLA Modules:
  0.0 41.9 jit_solution(823389938850364579)
XLA Ops:
  2.6 36.3 %shard_map.122 = (bf16[16,16,16,128]{3,2,1,0:T(8,128)(2,1)}, f32[1,32,128]{2,1,0:T(8,128)}) custom-call(bf16[16,16,16,128]{3,2,1,0:T(8,128)(2,1)} %wave_hbm.1, f32[16,256]{1,0:T(8,128)} %mass_hbm.1, f32[16,256]{1,0:T(8,128)} %pot_hbm.1, f32[2,2,2]{2,1,0:T(2,128)} %scale_hbm.1, bf16[729,729]{1,0:T(8,128)(2,1)} %stiff_hbm.1, bf16[1,32,729]{2,1,0:T(8,128)(2,1)} %bitcast.2, ...), custom_call_target="tpu_custom_call" | custom-call | tf_op jit(solution)/shard_map/pallas_call | solution.py:406
  38.8 0.0 copy-start
  38.9 2.4 %copy.18 = bf16[16,16,16,128]{3,2,1,0:T(8,128)(2,1)} copy(bf16[16,16,16,128]{3,2,1,0:T(8,128)(2,1)} %get-tuple-element.4) | data formatting | bytes 2097152
  41.3 0.0 copy-done
  41.3 0.6 %copy.19 = f32[1,32,128]{2,1,0:T(8,128)} copy(f32[1,32,128]{2,1,0:T(8,128)S(1)} %copy-done) | data formatting | bytes 32768
Async XLA Ops:
  38.8 2.4 %copy-start = (f32[1,32,128]{2,1,0:T(8,128)S(1)}, f32[1,32,128]{2,1,0:T(8,128)}, u32[]{:S(2)}) copy-start(f32[1,32,128]{2,1,0:T(8,128)} %get-tuple-element.5) | copy-start | bytes 49156

commit v3 on v2

--- a/solution.py
+++ b/solution.py
@@ -45,7 +45,7 @@
 
 
 def kernel(
-    wave_hbm, mass_hbm, pot_hbm, scale_hbm, stiff_hbm, lower_hbm, upper_hbm, kb_hbm, atom_col, count, upper_col,
+    wave_hbm, mass_hbm, pot_hbm, scale_hbm, stiff_hbm, lower_hbm, upper_hbm, kb_hbm, atom_ref, count_ref, next_ref,
     out_hbm, coef_hbm,
     wave, mass, pot, stiff, lower, upper, scale, kb, out_v, coef_v,
     sel, kp, both, both_t, massb, potb, mrim, wv, wf, rim, zl, stepv, pf, plane16, mass16, ez, e0,
@@ -57,6 +57,7 @@
     n = lax.axis_size("space")
     right, left = lax.rem(me + 1, n), lax.rem(me + n - 1, n)
     share = (1.0 / 6.0, 2.0 / 6.0)
+    atom_col, count, upper_col = atom_ref[0], count_ref[0], next_ref[0]
 
     barrier = pltpu.get_barrier_semaphore()
     for neighbour in (left, right):
@@ -66,10 +67,11 @@
     for slot, (source, target) in enumerate(
         [
             (mass_hbm, mass),
-            (wave_hbm, wave),
             (upper_hbm, upper),
             (lower_hbm, lower),
+            (wave_hbm.at[0:9], wave.at[0:9]),
             (stiff_hbm, stiff),
+            (wave_hbm.at[9:16], wave.at[9:16]),
             (pot_hbm, pot),
             (scale_hbm, scale),
             (kb_hbm, kb),
@@ -145,6 +147,10 @@
     loads[0].wait()
     spread(jnp.transpose(mass[...]), massb, range(16))
     loads[1].wait()
+    loads[2].wait()
+    turned = dot_turned(jnp.concatenate([upper[0], lower[0]], axis=0), sel[...])
+    both_t[...] = turned.astype(BF16)
+    loads[3].wait()
 
     def start_field(planes):
         for p in planes:
@@ -153,41 +159,40 @@
                     put_field(2 * a + b, p, massb[2 * a + b, p * 64 : p * 64 + 64] * block)
 
     def send_held_of(turn):
-        send_held[turn] = dot(both_t[0:CH], bottom_operand(upper_col[0]))
+        send_held[turn] = dot(both_t[0:CH], bottom_operand(upper_col))
         return remote(send_held.at[turn], a_held.at[turn], 3 + turn, left)
 
     start_field(range(0, 1))
     for ab in range(4):
         send_plane[0, ab] = wv[ab, 0:64]
+    start_field(range(1, 9))
+    build_rim(0)
+    send_held[0] = dot(both_t[0:CH], bottom_operand(upper_col))
     pl.semaphore_wait(barrier, 2)
     plane_copy = remote(send_plane.at[0], a_plane.at[0], 0, left)
-    loads[2].wait()
-    loads[3].wait()
-    turned = dot_turned(jnp.concatenate([upper[0], lower[0]], axis=0), sel[...])
-    both_t[...] = turned.astype(BF16)
-    start_field(range(1, 9))
-    build_rim(0)
-    held_copy = send_held_of(0)
+    held_copy = remote(send_held.at[0], a_held.at[0], 3, left)
     both[...] = jnp.transpose(jnp.concatenate([turned, jnp.zeros((64, DEPTH), F32)], axis=0)).astype(BF16)
     loads[4].wait()
-    half = dot(sel[...], stiff[...]).astype(BF16)
-    kp[...] = dot_turned(half, sel[...]).astype(BF16)
+    spans = [(0, 256, slice(0, 384)), (256, 512, slice(256, NODES)), (512, DEPTH, slice(0, NODES))]
+    half = jnp.concatenate([dot(sel[low:high, old], stiff[old]) for low, high, old in spans], axis=0).astype(BF16)
+    for low, high, old in spans:
+        kp[:, low:high] = dot_turned(half[:, old], sel[low:high, old]).astype(BF16)
     kp[:, COEF0:] = both[:, CH : 2 * CH]
+    for slot in (5, 6, 7, 8):
+        loads[slot].wait()
     start_field(range(9, 16))
-    for slot in (5, 6, 7):
-        loads[slot].wait()
     spread(jnp.transpose(pot[...]), potb, range(16))
 
     channel = lax.broadcasted_iota(jnp.int32, (CH, CH), 1)
     square = lax.broadcasted_iota(jnp.int32, (CH, CH), 0) == channel
-    live = jnp.logical_and(square, channel < count[0])
+    live = jnp.logical_and(square, channel < count)
     weight = jnp.sum(jnp.where(live, jnp.broadcast_to(kb[...], (CH, CH)), 0.0), axis=1, keepdims=True)
 
     def scale_of(layer, ab, rows):
         return jnp.broadcast_to(scale[layer, ab // 2 : ab // 2 + 1, ab % 2 : ab % 2 + 1], (rows, 128))
 
     def chosen(column, ab):
-        return jnp.where(column[0] == ab, 1.0, 0.0)
+        return jnp.where(column == ab, 1.0, 0.0)
 
     def layer_product(layer, rows, operands):
         for pair in range(2):
@@ -232,7 +237,7 @@
         for ab in range(4):
             mrim[ab, 160:192] = jnp.zeros((32, 128), F32)
         gather_rim(massb, 0, put)
-        at = upper_col[0]
+        at = upper_col
         node_mass = jnp.concatenate([massb[at, 0:MAIN], mrim[at]], axis=0)
         wide = both[...].astype(F32) * node_mass
         send_gram[0] = dot(both_t[0:CH], (wide * node_mass).astype(BF16)) * share[0]
@@ -241,8 +246,8 @@
         return sent
 
     def take_set_up(sent):
-        sent[0].wait_recv()
-        sent[1].wait_recv()
+        for copy in sent:
+            copy.wait_recv()
         wide = jnp.concatenate([a_edge[...].astype(F32), jnp.zeros((128 - CH, 256), F32)], axis=0)
         e0[...] = jnp.transpose(wide)[:, 0:CH].astype(BF16)
         spread(jnp.transpose(a_mass[...]), mass16, range(1))
@@ -264,12 +269,7 @@
         )
         return parts, held
 
-    def top_coef(turn, plane_copy, held_copy, setting):
-        if turn > 0:
-            if turn == 1:
-                take_set_up(setting)
-                setting[2].wait_recv()
-            parts, extra = finish_plane(turn)
+    def top_coef(turn, plane_copy, held_copy, parts, extra):
         plane_copy.wait_recv()
         for ab in range(4):
             value = a_plane[turn, ab].astype(F32)
@@ -281,7 +281,7 @@
             plane16[ab] = value
             wf[ab, 1024:1088] = value.astype(F32)
         build_rim(1)
-        own = dot(both_t[CH : 2 * CH], top_operand(atom_col[0]))
+        own = dot(both_t[CH : 2 * CH], top_operand(atom_col))
         held_copy.wait_recv()
         own = own + a_held[turn]
         return own if turn == 0 else own + extra
@@ -334,8 +334,8 @@
                         send_plane[turn + 1, ab] = value.astype(BF16)
                     put_field(ab, p, massb[ab, rows] * value if turn == 0 else value)
 
-    def bottom_planes(turn):
-        for p in range(9):
+    def bottom_planes(turn, planes):
+        for p in planes:
             for a in range(2):
                 values = []
                 for b in range(2):
@@ -347,12 +347,16 @@
                     values.append(pf[ab, rows] + massb[ab, rows] * share[turn] * extra)
                 keep(turn, p, a, values)
 
-    for turn in range(2):
+    def bottom_product():
         layer_product(0, [(0, COEF0)], [bottom_operand(ab) for ab in range(4)])
         layer_rims(0, range(9))
+
+    parts, extra = None, None
+    for turn in range(2):
         if turn == 0:
+            bottom_product()
             setting = set_up()
-        total = top_coef(turn, plane_copy, held_copy, setting) * weight
+        total = top_coef(turn, plane_copy, held_copy, parts, extra) * weight
         send_coef[turn] = total.astype(BF16)
         coef_copy = remote(send_coef.at[turn], b_coef.at[turn], 9 + turn, right)
         for ab in range(4):
@@ -364,6 +368,8 @@
         for ab in range(4):
             send_rim[turn, ab] = zl[1, ab, 512:576].astype(BF16)
         rim_copy = remote(send_rim.at[turn], b_rim.at[turn], 11 + turn, right)
+        if turn == 1:
+            bottom_product()
         layer_product(1, [(0, 512), (MAIN, 704)], operands)
         layer_rims(1, range(0, 8))
         bottom_planes_partly(turn)
@@ -374,26 +380,50 @@
         if turn == 1:
             early = pltpu.make_async_copy(out_v.at[9:16], out_hbm.at[9:16], store_sem.at[0])
             early.start()
+        if turn == 0:
+            take_set_up(setting)
+        parts, extra = finish_plane(turn + 1)
         coef_copy.wait_recv()
         spread_coef = dot(both[:COEF0, 0:CH], b_coef[turn])
         for ab in range(4):
             zl[0, ab, 0:COEF0] = spread_coef * chosen(upper_col, ab)
         layer_rims(0, range(9))
+        bottom_planes(turn, range(1, 9))
+        if turn == 1:
+            late = pltpu.make_async_copy(out_v.at[1:9], out_hbm.at[1:9], store_sem.at[1])
+            late.start()
         rim_copy.wait_recv()
-        bottom_planes(turn)
+        bottom_planes(turn, range(0, 1))
         if turn == 0:
             build_rim(0)
 
-    late = pltpu.make_async_copy(out_v.at[0:9], out_hbm.at[0:9], store_sem.at[1])
-    late.start()
-    coef_v[0] = top_coef(2, plane_copy, held_copy, setting)
+    first = pltpu.make_async_copy(out_v.at[0:1], out_hbm.at[0:1], store_sem.at[3])
+    first.start()
+    coef_v[0] = top_coef(2, plane_copy, held_copy, parts, extra)
     last = pltpu.make_async_copy(coef_v, coef_hbm, store_sem.at[2])
     last.start()
     for copy in copies:
         copy.wait_send()
     early.wait()
     late.wait()
+    first.wait()
     last.wait()
+
+
+def hand_on(field, coef, field_out, coef_out, held, coef_held, sem):
+    pairs = [(coef, coef_held, coef_out)]
+    for part in range(4):
+        planes = pl.ds(4 * part, 4)
+        pairs.append((field.at[planes], held.at[planes], field_out.at[planes]))
+    inward = [pltpu.make_async_copy(x, y, sem.at[k]) for k, (x, y, _) in enumerate(pairs)]
+    outward = [pltpu.make_async_copy(y, z, sem.at[5 + k]) for k, (_, y, z) in enumerate(pairs)]
+    for copy in inward:
+        copy.start()
+    for first, second in zip(inward, outward):
+        first.wait()
+        second.start()
+    for copy in outward:
+        copy.wait()
 
 
 def per_device(*arrays):
@@ -402,14 +432,13 @@
     arrays[5] = jnp.swapaxes(arrays[5], 1, 2)
     arrays[6] = jnp.swapaxes(arrays[6], 1, 2)
     any_space = pl.BlockSpec(memory_space=pl.ANY)
-    smem = pl.BlockSpec(memory_space=pltpu.SMEM)
-    return pl.pallas_call(
+    results = pl.pallas_call(
         kernel,
         out_shape=(
             jax.ShapeDtypeStruct(wave_in.shape, BF16),
             jax.ShapeDtypeStruct((1, CH, 128), F32),
         ),
-        in_specs=[any_space] * 8 + [smem] * 3,
+        in_specs=[any_space] * 8 + [pl.BlockSpec(memory_space=pltpu.SMEM)] * 3,
         out_specs=(any_space, any_space),
         scratch_shapes=[
             pltpu.VMEM((16, 16, 16, 128), BF16),
@@ -452,8 +481,8 @@
             pltpu.VMEM((2, CH, 128), F32),
             pltpu.VMEM((2, 4, 64, 128), BF16),
             pltpu.VMEM((2, CH, 128), BF16),
-            pltpu.SemaphoreType.DMA((8,)),
-            pltpu.SemaphoreType.DMA((3,)),
+            pltpu.SemaphoreType.DMA((9,)),
+            pltpu.SemaphoreType.DMA((4,)),
             pltpu.SemaphoreType.DMA((13,)),
             pltpu.SemaphoreType.DMA((13,)),
         ],
@@ -461,6 +490,20 @@
             collective_id=0, has_side_effects=True, vmem_limit_bytes=63 * 1024 * 1024
         ),
     )(*arrays)
+    return pl.pallas_call(
+        hand_on,
+        out_shape=(
+            jax.ShapeDtypeStruct(wave_in.shape, BF16),
+            jax.ShapeDtypeStruct((1, CH, 128), F32),
+        ),
+        in_specs=[any_space] * 2,
+        out_specs=(any_space, any_space),
+        scratch_shapes=[
+            pltpu.VMEM((16, 16, 16, 128), BF16),
+            pltpu.VMEM((1, CH, 128), F32),
+            pltpu.SemaphoreType.DMA((10,)),
+        ],
+    )(*results)
 
 
 def solution(mesh):

time: 42.1 us -> 40.4 us (0.960)
  local copies, waits for them, and re-layouts: 3.04 us -> 0 us
  Pallas kernels: 36.3 us -> 37.4 us
    unnamed x4 -> x0, local copies, waits for them, and re-layouts: 3.04 us -> none
    pallas_call x0 -> x1, Pallas kernels: none -> 2.02 us  [per_device(): pl.pallas_call(hand_on, out_shape=(jax.ShapeDtypeStruct(wave_in.shape, BF...]
    pallas_call x1, Pallas kernels: 36.3 us -> 35.4 us  [per_device(): pl.pallas_call(kernel, out_shape=(jax.ShapeDtypeStruct(wave_in.shape, BF1...]
where the time goes in v3:
time: 40.4 us; the launch traced here: 40 us
  Pallas kernels  37.4 us (93%)
  between operations  2.58 us (6%)
    pallas_call x1, Pallas kernels, per_device(): pl.pallas_call(kernel, out_shape=(jax.ShapeDtypeStruct(wave_in.shape, BF1...  35.4 us
    pallas_call x1, Pallas kernels, per_device(): pl.pallas_call(hand_on, out_shape=(jax.ShapeDtypeStruct(wave_in.shape, BF...  2.02 us

profile of v3, /device:TPU:8, one launch (start us, length us, event | category | flops | bytes accessed | tf_op | source)
XLA Modules:
  0.0 40.0 jit_solution(10213957730938674882)
XLA Ops:
  2.6 35.4 %shard_map.122 = (bf16[16,16,16,128]{3,2,1,0:T(8,128)(2,1)}, f32[1,32,128]{2,1,0:T(8,128)}) custom-call(bf16[16,16,16,128]{3,2,1,0:T(8,128)(2,1)} %wave_hbm.1, f32[16,256]{1,0:T(8,128)} %mass_hbm.1, f32[16,256]{1,0:T(8,128)} %pot_hbm.1, f32[2,2,2]{2,1,0:T(2,128)} %scale_hbm.1, bf16[729,729]{1,0:T(8,128)(2,1)} %stiff_hbm.1, bf16[1,32,729]{2,1,0:T(8,128)(2,1)} %bitcast.2, ...), custom_call_target="tpu_custom_call" | custom-call | tf_op jit(solution)/shard_map/pallas_call | solution.py:435
  38.0 2.0 %shard_map.123 = (bf16[16,16,16,128]{3,2,1,0:T(8,128)(2,1)}, f32[1,32,128]{2,1,0:T(8,128)}) custom-call(bf16[16,16,16,128]{3,2,1,0:T(8,128)(2,1)} %get-tuple-element.4.field, f32[1,32,128]{2,1,0:T(8,128)} %get-tuple-element.5.coef), custom_call_target="tpu_custom_call" | custom-call | tf_op jit(solution)/shard_map/pallas_call | solution.py:493

commit v4 on v3

--- a/solution.py
+++ b/solution.py
@@ -369,6 +369,10 @@
             send_rim[turn, ab] = zl[1, ab, 512:576].astype(BF16)
         rim_copy = remote(send_rim.at[turn], b_rim.at[turn], 11 + turn, right)
         if turn == 1:
+            bottom_planes(0, range(1, 8))
+            before_rim.wait_recv()
+            bottom_planes(0, range(0, 1))
+            build_rim(0)
             bottom_product()
         layer_product(1, [(0, 512), (MAIN, 704)], operands)
         layer_rims(1, range(0, 8))
@@ -388,14 +392,15 @@
         for ab in range(4):
             zl[0, ab, 0:COEF0] = spread_coef * chosen(upper_col, ab)
         layer_rims(0, range(9))
-        bottom_planes(turn, range(1, 9))
-        if turn == 1:
+        if turn == 0:
+            bottom_planes(turn, range(8, 9))
+            before_rim = rim_copy
+        else:
+            bottom_planes(turn, range(1, 9))
             late = pltpu.make_async_copy(out_v.at[1:9], out_hbm.at[1:9], store_sem.at[1])
             late.start()
-        rim_copy.wait_recv()
-        bottom_planes(turn, range(0, 1))
-        if turn == 0:
-            build_rim(0)
+    rim_copy.wait_recv()
+    bottom_planes(1, range(0, 1))
 
     first = pltpu.make_async_copy(out_v.at[0:1], out_hbm.at[0:1], store_sem.at[3])
     first.start()

time: 40.4 us -> 40.4 us (level)
  the two profiles are of different devices: /device:TPU:8 before, /device:TPU:16 now
where the time goes in v4:
time: 40.4 us; the launch traced here: 40 us
  Pallas kernels  37.4 us (93%)
  between operations  2.58 us (6%)
    pallas_call x1, Pallas kernels, per_device(): pl.pallas_call(kernel, out_shape=(jax.ShapeDtypeStruct(wave_in.shape, BF1...  35.4 us
    pallas_call x1, Pallas kernels, per_device(): pl.pallas_call(hand_on, out_shape=(jax.ShapeDtypeStruct(wave_in.shape, BF...  2.02 us

profile of v4, /device:TPU:16, one launch (start us, length us, event | category | flops | bytes accessed | tf_op | source)
XLA Modules:
  0.0 40.0 jit_solution(18086639483147419939)
XLA Ops:
  2.6 35.4 %shard_map.122 = (bf16[16,16,16,128]{3,2,1,0:T(8,128)(2,1)}, f32[1,32,128]{2,1,0:T(8,128)}) custom-call(bf16[16,16,16,128]{3,2,1,0:T(8,128)(2,1)} %wave_hbm.1, f32[16,256]{1,0:T(8,128)} %mass_hbm.1, f32[16,256]{1,0:T(8,128)} %pot_hbm.1, f32[2,2,2]{2,1,0:T(2,128)} %scale_hbm.1, bf16[729,729]{1,0:T(8,128)(2,1)} %stiff_hbm.1, bf16[1,32,729]{2,1,0:T(8,128)(2,1)} %bitcast.2, ...), custom_call_target="tpu_custom_call" | custom-call | tf_op jit(solution)/shard_map/pallas_call | solution.py:440
  38.0 2.0 %shard_map.123 = (bf16[16,16,16,128]{3,2,1,0:T(8,128)(2,1)}, f32[1,32,128]{2,1,0:T(8,128)}) custom-call(bf16[16,16,16,128]{3,2,1,0:T(8,128)(2,1)} %get-tuple-element.4.field, f32[1,32,128]{2,1,0:T(8,128)} %get-tuple-element.5.coef), custom_call_target="tpu_custom_call" | custom-call | tf_op jit(solution)/shard_map/pallas_call | solution.py:498

commit v5 on v3

--- a/solution.py
+++ b/solution.py
@@ -388,7 +388,12 @@
         for ab in range(4):
             zl[0, ab, 0:COEF0] = spread_coef * chosen(upper_col, ab)
         layer_rims(0, range(9))
-        bottom_planes(turn, range(1, 9))
+        bottom_planes(turn, range(8, 9))
+        if turn == 1:
+            coef_v[0] = top_coef(2, plane_copy, held_copy, parts, extra)
+            last = pltpu.make_async_copy(coef_v, coef_hbm, store_sem.at[2])
+            last.start()
+        bottom_planes(turn, range(1, 8))
         if turn == 1:
             late = pltpu.make_async_copy(out_v.at[1:9], out_hbm.at[1:9], store_sem.at[1])
             late.start()
@@ -399,9 +404,6 @@
 
     first = pltpu.make_async_copy(out_v.at[0:1], out_hbm.at[0:1], store_sem.at[3])
     first.start()
-    coef_v[0] = top_coef(2, plane_copy, held_copy, parts, extra)
-    last = pltpu.make_async_copy(coef_v, coef_hbm, store_sem.at[2])
-    last.start()
     for copy in copies:
         copy.wait_send()
     early.wait()
@@ -412,11 +414,11 @@
 
 def hand_on(field, coef, field_out, coef_out, held, coef_held, sem):
     pairs = [(coef, coef_held, coef_out)]
-    for part in range(4):
-        planes = pl.ds(4 * part, 4)
+    for part in range(8):
+        planes = pl.ds(2 * part, 2)
         pairs.append((field.at[planes], held.at[planes], field_out.at[planes]))
     inward = [pltpu.make_async_copy(x, y, sem.at[k]) for k, (x, y, _) in enumerate(pairs)]
-    outward = [pltpu.make_async_copy(y, z, sem.at[5 + k]) for k, (_, y, z) in enumerate(pairs)]
+    outward = [pltpu.make_async_copy(y, z, sem.at[9 + k]) for k, (_, y, z) in enumerate(pairs)]
     for copy in inward:
         copy.start()
     for first, second in zip(inward, outward):
@@ -501,7 +503,7 @@
         scratch_shapes=[
             pltpu.VMEM((16, 16, 16, 128), BF16),
             pltpu.VMEM((1, CH, 128), F32),
-            pltpu.SemaphoreType.DMA((10,)),
+            pltpu.SemaphoreType.DMA((18,)),
         ],
     )(*results)
 

time: 40.4 us -> 40.2 us (level)
  no operation moved by 1% of the time
where the time goes in v5:
time: 40.2 us; the launch traced here: 39.9 us
  Pallas kernels  37.3 us (93%)
  between operations  2.58 us (6%)
    pallas_call x1, Pallas kernels, per_device(): pl.pallas_call(kernel, out_shape=(jax.ShapeDtypeStruct(wave_in.shape, BF1...  35.2 us
    pallas_call x1, Pallas kernels, per_device(): pl.pallas_call(hand_on, out_shape=(jax.ShapeDtypeStruct(wave_in.shape, BF...  2.12 us

profile of v5, /device:TPU:8, one launch (start us, length us, event | category | flops | bytes accessed | tf_op | source)
XLA Modules:
  0.0 39.9 jit_solution(3520850944034635493)
XLA Ops:
  2.6 35.2 %shard_map.122 = (bf16[16,16,16,128]{3,2,1,0:T(8,128)(2,1)}, f32[1,32,128]{2,1,0:T(8,128)}) custom-call(bf16[16,16,16,128]{3,2,1,0:T(8,128)(2,1)} %wave_hbm.1, f32[16,256]{1,0:T(8,128)} %mass_hbm.1, f32[16,256]{1,0:T(8,128)} %pot_hbm.1, f32[2,2,2]{2,1,0:T(2,128)} %scale_hbm.1, bf16[729,729]{1,0:T(8,128)(2,1)} %stiff_hbm.1, bf16[1,32,729]{2,1,0:T(8,128)(2,1)} %bitcast.2, ...), custom_call_target="tpu_custom_call" | custom-call | tf_op jit(solution)/shard_map/pallas_call | solution.py:437
  37.8 2.1 %shard_map.123 = (bf16[16,16,16,128]{3,2,1,0:T(8,128)(2,1)}, f32[1,32,128]{2,1,0:T(8,128)}) custom-call(bf16[16,16,16,128]{3,2,1,0:T(8,128)(2,1)} %get-tuple-element.4.field, f32[1,32,128]{2,1,0:T(8,128)} %get-tuple-element.5.coef), custom_call_target="tpu_custom_call" | custom-call | tf_op jit(solution)/shard_map/pallas_call | solution.py:495
